TPU v7x, 32 devices: a whole 2x2x4 slice. The times are simulated.
32 devices in a mesh: groups: 2 (over y), replica: 4 (over z), tensor: 4 (over x, core).
Axes of the slice: x: 2, y: 2, z: 4, core: 2. Of those that a mesh axis runs over, the one named last changes fastest.
Arguments:
- hidden: bfloat16 [64, 2, 8192], P(('groups', 'replica')), parts along dimension 0, may hold values from -6 to 6
- queries: bfloat16 [64, 2, 8192], P(('groups', 'replica'), None, 'tensor'), parts along dimension 0, may hold values from -60 to 60
- earlier_token_cache: bfloat16 [64, 2, 512, 1024], P(('groups', 'replica'), None, None, 'tensor'), parts along dimension 0, may hold values from -6 to 6
- lengths: int32 [8, 8], P(('groups', 'replica')), parts along dimension 0, may hold values from 1 to 3, 17 in all within a row
- request_hot_entry: int32 [64], P(('groups', 'replica')), parts along dimension 0, may hold values from 0 to 1
- destination: int32 [64], P(('groups', 'replica')), parts along dimension 0, may hold values from 0 to 3, as said below
- placement: int32 [4], P('groups'), parts along dimension 0, may hold values from 0 to 3
- base_key_value_weight: bfloat16 [8192, 2, 1024], P(None, None, 'tensor'), may hold values from -0.0625 to 0.0625
- adapter_first_factors: bfloat16 [4, 8192, 256], P('replica', 'tensor'), may hold values from -0.0625 to 0.0625
- adapter_second_factors: bfloat16 [4, 2, 128, 1024], P('replica', None, None, 'tensor'), may hold values from -0.5 to 0.5
Outputs:
- moved_cache: bfloat16 [64, 2, 512, 1024], P(('groups', 'replica'), None, None, 'tensor'), parts along dimension 0
- moved_attention: bfloat16 [64, 2, 8192], P(('groups', 'replica'), None, 'tensor'), parts along dimension 0
- resident_first_factors: bfloat16 [4, 8192, 256], P('groups', 'tensor'), parts along dimension 0
- resident_second_factors: bfloat16 [4, 2, 128, 1024], P('groups', None, None, 'tensor'), parts along dimension 0
There are 2 independent parts, one for each index of `groups`. A program takes and returns all parts, laid end to end along the dimension named above; an argument that names none is the same for every part. Nothing has to cross between parts.
Inputs may be any that keep to these rules, and one draw needn't show every extreme that they name: Each replica's 8 lengths sum to 17 blocks, and one of them is 3. A request's adapter is placement[request_hot_entry]. `placement`: entries may repeat. `destination`: each replica's requests name any one replica at most 2 times, and one replica is named exactly 2 times by the requests of every replica.
All inputs are finite; a program needn't handle non-finite values.
Results may differ from a plain program's by a relative error of at most 0.0052.
Values may be sent and summed in bfloat16 or wider, within the bound.
No kernel may reach another device: no remote copies, remote signals or barrier semaphores. Data moves between devices by JAX's collectives and lax.ppermute only.
A program may use at most 128 MiB of HBM per device.

v0:
```python
import functools

import jax
import jax.numpy as jnp
from jax import lax
from jax.experimental import pallas as pl
from jax.experimental.pallas import tpu as pltpu
from jax.sharding import PartitionSpec as P

HEAD_WIDTH = 128
BLOCK = 128
TILE = 16
LANES = 128
SMEM = pl.BlockSpec(memory_space=pltpu.SMEM)
VMEM = pl.BlockSpec(memory_space=pltpu.VMEM)
CHEAP = pl.CostEstimate(flops=1, bytes_accessed=1, transcendentals=0)
HBM = pl.BlockSpec(memory_space=pltpu.HBM)


def exchange(values, axis, mask):
    size = lax.axis_size(axis)
    return lax.ppermute(values, axis, [(i, i ^ mask) for i in range(size)])


def gate_kernel(*refs):
    pass


def gate(values, *after):
    return pl.pallas_call(
        gate_kernel,
        out_shape=[jax.ShapeDtypeStruct(v.shape, v.dtype) for v in values],
        in_specs=[HBM] * (len(values) + len(after)),
        out_specs=[HBM] * len(values),
        input_output_aliases={i: i for i in range(len(values))},
        cost_estimate=CHEAP,
        name="gate",
    )(*values, *after)


def pack_kernel(layout, live, me_ref, dest_ref, count_ref, cache_ref, *rest):
    outs = rest[: len(layout)]
    mark_ref, stage, in_sems, out_sems = rest[len(layout) :]
    mark_ref[...] = jnp.zeros_like(mark_ref)
    requests = dest_ref.shape[0]
    me = me_ref[0]
    moves = []
    for r in range(requests):
        blocks, target = count_ref[r], dest_ref[r]
        offset = jnp.int32(0)
        for earlier in range(r):
            offset = offset + jnp.where(dest_ref[earlier] == target, count_ref[earlier], 0)
        for b in range(live):
            index = r * live + b
            going = (b < blocks) & (target != me)
            position = offset + b
            inward = pltpu.make_async_copy(
                cache_ref.at[r, :, pl.ds(b * BLOCK, BLOCK), :], stage.at[index], in_sems.at[index]
            )
            outward = []
            for (pattern, first, amount), out_ref in zip(layout, outs):
                here = position - first
                outward.append(
                    (
                        going & (target == (me ^ pattern)) & (here >= 0) & (here < amount),
                        pltpu.make_async_copy(
                            stage.at[index],
                            out_ref.at[jnp.clip(here, 0, amount - 1)],
                            out_sems.at[index],
                        ),
                    )
                )
            moves.append((going, inward, outward))
    for going, inward, _ in moves:
        pl.when(going)(inward.start)
    for going, inward, outward in moves:
        pl.when(going)(inward.wait)
        for this, copy in outward:
            pl.when(this)(copy.start)
    for going, _, outward in moves:
        pl.when(going)(outward[0][1].wait)


def pack(me, destination, counts, cache, layout):
    requests, _, context, width = cache.shape
    live = context // BLOCK - 1
    return pl.pallas_call(
        functools.partial(pack_kernel, layout, live),
        out_shape=[
            jax.ShapeDtypeStruct((amount, 2, BLOCK, width), cache.dtype)
            for _, _, amount in layout
        ]
        + [jax.ShapeDtypeStruct((8, LANES), jnp.float32)],
        in_specs=[SMEM, SMEM, SMEM, HBM],
        out_specs=[HBM] * len(layout) + [VMEM],
        scratch_shapes=[
            pltpu.VMEM((requests * live, 2, BLOCK, width), cache.dtype),
            pltpu.SemaphoreType.DMA((requests * live,)),
            pltpu.SemaphoreType.DMA((requests * live,)),
        ],
        compiler_params=pltpu.CompilerParams(vmem_limit_bytes=60 << 20),
        cost_estimate=CHEAP,
        name="pack",
    )(me, destination, counts, cache)


def unpack_kernel(layout, own, fill, tail, pairs, live, *refs):
    me_ref, dest_ref, count_ref = refs[:3]
    at = 3
    if own:
        cache_ref = refs[at]
        at += 1
    received = refs[at : at + len(layout)]
    at += len(layout)
    replicas, requests = dest_ref.shape
    if tail:
        small_ref = refs[at]
        at += 1
    if not fill:
        at += 2
    out_ref = refs[at]
    at += 1
    if tail:
        att_ref = refs[at]
        at += 1
    sems = refs[at]
    at += 1
    if own:
        own_stage, own_sems = refs[at : at + 2]
        at += 2
    if fill:
        zero_ref = refs[at]
        at += 1
        zero_ref[...] = jnp.zeros_like(zero_ref)
    if tail:
        stage_ref = refs[at]
    width = out_ref.shape[3]
    me = me_ref[0]
    copies, moves = [], []
    used = 0

    def copy_to(source, target):
        nonlocal used
        used += 1
        return pltpu.make_async_copy(source, target, sems.at[used - 1])

    slot_info = []
    for pattern in range(replicas):
        source_replica = me ^ pattern
        arrived = jnp.int32(0)
        offset = jnp.int32(0)
        lengths_of = [jnp.int32(-1)] * pairs
        for r in range(requests):
            mine = dest_ref[pattern, r] == me
            blocks = count_ref[pattern, r]
            slot = source_replica * pairs + jnp.minimum(arrived, pairs - 1)
            for b in range(live):
                place = pl.ds(b * BLOCK, BLOCK)
                target = out_ref.at[slot, :, place, :]
                valid = mine & (b < blocks)
                if pattern == 0 and own:
                    index = r * live + b
                    inward = pltpu.make_async_copy(
                        cache_ref.at[r, :, place, :], own_stage.at[index], own_sems.at[index]
                    )
                    moves.append((valid, inward, [(valid, copy_to(own_stage.at[index], target))]))
                for (of, first, amount), received_ref in zip(layout, received):
                    if of == pattern:
                        here = offset + b - first
                        source = received_ref.at[jnp.clip(here, 0, amount - 1)]
                        inside = valid & (here >= 0) & (here < amount)
                        copies.append((inside, copy_to(source, target)))
            lengths_of = [
                jnp.where(mine & (arrived == k), blocks, lengths_of[k]) for k in range(pairs)
            ]
            arrived = arrived + jnp.where(mine, 1, 0)
            offset = offset + jnp.where(mine, blocks, 0)
        for k in range(pairs):
            slot_info.append((pattern, k, source_replica * pairs + k, lengths_of[k]))
    if fill:
        for pattern, k, slot, blocks in slot_info:
            for b in range(live + 1):
                target = out_ref.at[slot, :, pl.ds(b * BLOCK, BLOCK), :]
                copies.append((b >= blocks, copy_to(zero_ref, target)))
    for condition, inward, _ in moves:
        pl.when(condition)(inward.start)
    for condition, copy in copies:
        pl.when(condition)(copy.start)
    if tail:
        rows = lax.broadcasted_iota(jnp.int32, (TILE, LANES), 0)
        heads = width // LANES
        for index, (pattern, k, slot, blocks) in enumerate(slot_info):
            small = small_ref[me ^ pattern, k]
            filled = blocks >= 0
            att_ref[slot] = jnp.where(filled, small[:, :width], jnp.zeros((), small.dtype))
            fresh = small[:, width:].astype(jnp.float32)
            for kv in range(2):
                for head in range(heads):
                    at_row = 2 * (kv * heads + head)
                    moved = pltpu.roll(fresh, (TILE - at_row) % TILE, 0)
                    stage_ref[index, kv, :, pl.ds(head * LANES, LANES)] = jnp.where(
                        rows < 2, moved, 0.0
                    ).astype(jnp.bfloat16)
            start = pl.multiple_of(jnp.maximum(blocks, 0) * BLOCK, BLOCK)
            copy = copy_to(stage_ref.at[index], out_ref.at[slot, :, pl.ds(start, TILE), :])
            pl.when(filled)(copy.start)
            copies.append((filled, copy))
    for condition, inward, outward in moves:
        pl.when(condition)(inward.wait)
        for going, copy in outward:
            pl.when(going)(copy.start)
            copies.append((going, copy))
    for condition, copy in copies:
        pl.when(condition)(copy.wait)


def unpack(me, dest_all, count_all, cache, received, smalls, out, pairs, context, after):
    replicas, requests = dest_all.shape
    own, fill, tail = cache is not None, out is None, smalls is not None
    layout = tuple(sorted(received))
    like = cache if own else received[layout[0]]
    dtype, width = like.dtype, like.shape[-1]
    live = context // BLOCK - 1
    slots = replicas * pairs
    args, specs = [me, dest_all, count_all], [SMEM] * 3
    if own:
        args.append(cache)
        specs.append(HBM)
    for part in layout:
        args.append(received[part])
        specs.append(VMEM)
    if tail:
        args.append(smalls)
        specs.append(VMEM)
    aliases = {}
    if not fill:
        aliases = {len(args): 0}
        args += [out, after]
        specs += [HBM] * 2
    out_shape = [jax.ShapeDtypeStruct((slots, 2, context, width), dtype)]
    out_specs = [HBM]
    amount = (len(layout) + (1 if own else 0)) * requests * live
    scratch = []
    if own:
        scratch.append(pltpu.VMEM((requests * live, 2, BLOCK, width), dtype))
        scratch.append(pltpu.SemaphoreType.DMA((requests * live,)))
    if fill:
        amount += slots * (live + 1)
        scratch.append(pltpu.VMEM((2, BLOCK, width), dtype))
    if tail:
        amount += slots
        out_shape.append(jax.ShapeDtypeStruct((slots, TILE, width), dtype))
        out_specs.append(VMEM)
        scratch.append(pltpu.VMEM((slots, 2, TILE, width), dtype))
    return pl.pallas_call(
        functools.partial(unpack_kernel, layout, own, fill, tail, pairs, live),
        out_shape=out_shape,
        in_specs=specs,
        out_specs=out_specs,
        scratch_shapes=[pltpu.SemaphoreType.DMA((amount,))] + scratch,
        input_output_aliases=aliases,
        compiler_params=pltpu.CompilerParams(vmem_limit_bytes=60 << 20),
        cost_estimate=CHEAP,
        name="unpack_tail" if tail else "unpack",
    )(*args)


def adapt_kernel(half, extra, amount, me_ref, own_ref, other_ref, group_ref, ids_ref, tokens_ref, *refs):
    pieces = refs[:amount]
    first_ref, second_ref, first_send_ref, second_send_ref, product_ref, sems = refs[amount + 1 :]
    me, group = me_ref[0], group_ref[0]
    copies = []

    def add(condition, source, target):
        copies.append((condition, pltpu.make_async_copy(source, target, sems.at[len(copies)])))

    for h in range(own_ref.shape[0]):
        for mask, piece in enumerate(pieces):
            other = (other_ref[h] ^ me) == mask
            add(other, piece.at[pl.ds(half, extra), :], second_send_ref.at[h])
            add(other, piece.at[pl.ds(0, half), :], first_send_ref.at[h])
            mine = (own_ref[h] ^ me) == mask
            add(mine, piece.at[pl.ds(half, extra), :], second_ref.at[h])
            start = pl.multiple_of(group * half, half)
            add(mine, piece.at[pl.ds(0, half), :], first_ref.at[h, pl.ds(start, half), :])
    for condition, copy in copies:
        pl.when(condition)(copy.start)
    total = jnp.zeros(product_ref.shape, jnp.float32)
    for mask, piece in enumerate(pieces):
        product = jnp.dot(
            tokens_ref[...], piece[pl.ds(0, half), :], preferred_element_type=jnp.float32
        )
        total = total + jnp.where(ids_ref[...] == (me ^ mask), product, 0.0)
    product_ref[...] = total
    for condition, copy in copies:
        pl.when(condition)(copy.wait)


def adapt(me, group, placement, other_placement, ids, tokens, pieces, half, extra, after):
    hot = placement.shape[0]
    rank2 = pieces[0].shape[1]
    dtype = pieces[0].dtype
    return pl.pallas_call(
        functools.partial(adapt_kernel, half, extra, len(pieces)),
        out_shape=[
            jax.ShapeDtypeStruct((hot, 2 * half, rank2), dtype),
            jax.ShapeDtypeStruct((hot, extra, rank2), dtype),
            jax.ShapeDtypeStruct((hot, half, rank2), dtype),
            jax.ShapeDtypeStruct((hot, extra, rank2), dtype),
            jax.ShapeDtypeStruct((tokens.shape[0], rank2), jnp.float32),
        ],
        in_specs=[SMEM] * 4 + [VMEM] * (2 + len(pieces)) + [HBM],
        out_specs=[HBM] * 4 + [VMEM],
        scratch_shapes=[pltpu.SemaphoreType.DMA((4 * hot * len(pieces),))],
        compiler_params=pltpu.CompilerParams(vmem_limit_bytes=60 << 20),
        cost_estimate=CHEAP,
        name="adapt",
    )(me, placement, other_placement, group, ids, tokens, *pieces, after)


def place_kernel(group_ref, received_ref, _, out_ref, sem):
    half = received_ref.shape[1]
    start = pl.multiple_of((1 - group_ref[0]) * half, half)
    copy = pltpu.make_async_copy(received_ref, out_ref.at[:, pl.ds(start, half), :], sem)
    copy.start()
    copy.wait()


def place_half(group, received, out):
    return pl.pallas_call(
        place_kernel,
        out_shape=jax.ShapeDtypeStruct(out.shape, out.dtype),
        in_specs=[SMEM, VMEM, HBM],
        out_specs=HBM,
        scratch_shapes=[pltpu.SemaphoreType.DMA],
        compiler_params=pltpu.CompilerParams(vmem_limit_bytes=60 << 20),
        input_output_aliases={2: 0},
        cost_estimate=CHEAP,
        name="place_half",
    )(group, received, out)


def attend_kernel(
    place_ref, count_ref, hot_ref, low_ref, second_ref, base_ref, cos_ref, sin_ref, query_ref,
    cache_ref, _, out_ref,
):
    r = pl.program_id(0)
    start = count_ref[r] * BLOCK
    entry = hot_ref[r]
    rank = second_ref.shape[2]
    width = cache_ref.shape[3]
    context = cache_ref.shape[2]
    heads = width // LANES
    low = low_ref[0]
    base = base_ref[0]
    delta_key = jnp.dot(low[:, :rank], second_ref[entry, 0], preferred_element_type=jnp.float32)
    delta_value = jnp.dot(low[:, rank:], second_ref[entry, 1], preferred_element_type=jnp.float32)
    key_pre = base[:, :width] + delta_key
    new_value = (base[:, width:] + delta_value).astype(jnp.bfloat16)
    columns = lax.broadcasted_iota(jnp.int32, (TILE, context), 1)
    second_token = lax.broadcasted_iota(jnp.int32, (TILE, 1), 0) >= TILE // 2
    fresh_keys, fresh_values = [], []
    for head in range(heads):
        lanes = slice(head * LANES, (head + 1) * LANES)
        k = key_pre[:, lanes]
        swapped = pltpu.roll(k, LANES // 2, 1)
        new_key = (k * cos_ref[0] + swapped * sin_ref[0]).astype(jnp.bfloat16).astype(jnp.float32)
        value_rows = new_value[:, lanes].astype(jnp.float32)
        fresh_keys.append(new_key)
        fresh_values.append(value_rows)
        q = query_ref[0, head]
        qf = q.astype(jnp.float32)
        scale = HEAD_WIDTH ** (-0.5)
        scores = lax.dot_general(
            q, cache_ref[0, 0, :, lanes], (((1,), (1,)), ((), ())),
            preferred_element_type=jnp.float32,
        ) * scale
        scores = jnp.where(columns < start, scores, -1e30)
        s0 = jnp.sum(qf * new_key[0:1], -1, keepdims=True) * scale
        s1 = jnp.sum(qf * new_key[1:2], -1, keepdims=True) * scale
        s1 = jnp.where(second_token, s1, -1e30)
        top = jnp.maximum(jnp.max(scores, -1, keepdims=True), jnp.maximum(s0, s1))
        weights = jnp.exp(scores - top)
        w0 = jnp.exp(s0 - top)
        w1 = jnp.exp(s1 - top)
        total = jnp.sum(weights, -1, keepdims=True) + w0 + w1
        probs = (weights / total).astype(jnp.bfloat16)
        p0 = (w0 / total).astype(jnp.bfloat16).astype(jnp.float32)
        p1 = (w1 / total).astype(jnp.bfloat16).astype(jnp.float32)
        attended = jnp.dot(
            probs, cache_ref[0, 1, :, lanes], preferred_element_type=jnp.float32
        )
        attended = attended + p0 * value_rows[0:1] + p1 * value_rows[1:2]
        out_ref[0, :, lanes] = attended.astype(jnp.bfloat16)
    fresh = fresh_keys + fresh_values
    if 2 * len(fresh) < TILE:
        fresh.append(jnp.zeros((TILE - 2 * len(fresh), LANES), jnp.float32))
    out_ref[0, :, width:] = jnp.concatenate(fresh, 0).astype(jnp.bfloat16)


def attend(place, counts, hot, low, second, base, cos, sin, query, cache, slots, after):
    requests, _, context, width = cache.shape
    heads = width // LANES

    def by_request(shape):
        return pl.BlockSpec((1,) + shape, lambda r, p, c, h: (r,) + (0,) * len(shape))

    return pl.pallas_call(
        attend_kernel,
        out_shape=jax.ShapeDtypeStruct((slots, TILE, width + LANES), cache.dtype),
        grid_spec=pltpu.PrefetchScalarGridSpec(
            num_scalar_prefetch=3,
            grid=(requests,),
            in_specs=[
                by_request((2, low.shape[2])),
                pl.BlockSpec(second.shape, lambda r, p, c, h: (0, 0, 0, 0)),
                by_request((2, 2 * width)),
                by_request((2, LANES)),
                by_request((2, LANES)),
                by_request((heads, TILE, LANES)),
                by_request((2, context, width)),
                HBM,
            ],
            out_specs=pl.BlockSpec((1, TILE, width + LANES), lambda r, p, c, h: (p[r], 0, 0)),
        ),
        cost_estimate=CHEAP,
        name="attend",
    )(place, counts, hot, low, second, base, cos, sin, query, cache, after)


def per_device(
    hidden,
    queries,
    earlier_token_cache,
    lengths,
    request_hot_entry,
    destination,
    placement,
    base_key_value_weight,
    adapter_first_factors,
    adapter_second_factors,
):
    replicas = lax.axis_size("replica")
    tensor = lax.axis_size("tensor")
    replica = lax.axis_index("replica").astype(jnp.int32)
    group = lax.axis_index("groups").astype(jnp.int32)
    part = lax.axis_index("tensor").astype(jnp.int32)
    requests = hidden.shape[0]
    pairs = max(1, requests // replicas)
    context, width = earlier_token_cache.shape[2:]
    heads = width // LANES
    live = context // BLOCK - 1
    piece = adapter_first_factors.shape[1]
    half = piece // 2
    rank2 = adapter_first_factors.shape[2]
    rank = rank2 // 2
    hot = placement.shape[0]
    me = replica[None]
    group_at = group[None]
    counts = lengths.reshape(-1)

    first_half = lax.dynamic_slice_in_dim(adapter_first_factors[0], group * half, half, 0)
    second_half = lax.dynamic_index_in_dim(
        adapter_second_factors[0], group, 0, keepdims=False
    ).reshape(-1, rank2)
    extra = second_half.shape[0]
    info = jnp.concatenate([counts, destination]).astype(jnp.bfloat16)
    info = jnp.pad(info[None], ((0, TILE - 1), (0, rank2 - info.shape[0])))
    pieces = {0: jnp.concatenate([first_half, second_half, info], 0)}
    bit = replicas // 2
    while bit:
        for mask in list(pieces):
            pieces[mask ^ bit] = exchange(pieces[mask], "replica", bit)
        bit //= 2
    pieces = [pieces[mask] for mask in range(replicas)]
    infos = jnp.stack([p[half + extra, : 2 * requests] for p in pieces]).astype(jnp.int32)
    count_all, dest_all = infos[:, :requests], infos[:, requests:]

    cap = live * pairs
    patterns = tuple(range(1, replicas))
    layout = tuple((p, 0, cap) for p in patterns)
    *packed, mark = pack(me, destination, counts, earlier_token_cache, layout)
    packed = dict(zip(layout, packed))

    tokens = hidden.reshape(requests * 2, -1)
    ids = jnp.repeat(placement[request_hot_entry], 2)
    notes = jnp.concatenate(
        [ids[:, None], jnp.broadcast_to(placement[None], (requests * 2, hot))], 1
    ).astype(jnp.bfloat16)
    notes = jnp.pad(notes, ((0, 0), (0, LANES - 1 - hot)))
    theirs = lax.dynamic_slice_in_dim(tokens, part * piece + (1 - group) * half, half, 1)
    (theirs,) = gate([jnp.concatenate([theirs, notes], 1)], mark)
    theirs = exchange(theirs, "groups", 1)
    other_ids = theirs[:, half].astype(jnp.int32)
    other_placement = theirs[0, half + 1 : half + 1 + hot].astype(jnp.int32)
    ours = lax.dynamic_slice_in_dim(tokens, part * piece + group * half, half, 1)
    both = jnp.concatenate([ours, theirs[:, :half]], 0)
    both_ids = jnp.broadcast_to(
        jnp.concatenate([ids, other_ids])[:, None], (4 * requests, rank2)
    )
    base = jnp.einsum(
        "ntd,dkc->ntkc", hidden, base_key_value_weight, preferred_element_type=jnp.float32
    ).reshape(requests, 2, 2 * width)
    received = {}
    first_parts = layout
    ready = gate(
        [packed[part] for part in first_parts],
        pieces[replicas // 2], pieces[1], both, both_ids, base,
    )
    for part, values in zip(first_parts, ready):
        received[part] = exchange(values, "replica", part[0])
    always = counts[0] > 0

    positions = (BLOCK * counts)[:, None] + jnp.arange(2)[None, :]
    half_size = HEAD_WIDTH // 2
    frequency = 10000.0 ** (-(jnp.arange(half_size, dtype=jnp.float32) * 2.0 / HEAD_WIDTH))
    angles = positions.astype(jnp.float32)[..., None] * frequency
    cos, sin = jnp.cos(angles), jnp.sin(angles)
    cos = jnp.concatenate([cos, cos], -1)
    sin = jnp.concatenate([-sin, sin], -1)
    group_size = queries.shape[2] // width
    query = (
        queries.reshape(requests, 2, heads, group_size, HEAD_WIDTH)
        .transpose(0, 2, 1, 3, 4)
        .reshape(requests, heads, 2 * group_size, HEAD_WIDTH)
    )
    order = jnp.arange(requests)
    same = destination[:, None] == destination[None, :]
    arrival = jnp.sum((same & (order[None, :] < order[:, None])).astype(jnp.int32), 1)
    place = destination * pairs + arrival
    slots = replicas * pairs

    def serve():
        first, second, first_send, second_send, products = adapt(
            me, group_at, placement, other_placement, both_ids, both, pieces, half, extra, both
        )
        low = products[: 2 * requests] + exchange(products[2 * requests :], "groups", 1)
        second_other = exchange(second_send, "groups", 1)
        (first_send,) = gate([first_send], low, second_other)
        first_other = exchange(first_send, "groups", 1)
        resident_first = place_half(group_at, first_other, first)
        theirs = second_other.reshape(hot, rank, width)
        bit = 1
        while bit < tensor:
            low = low + exchange(low, "tensor", bit)
            bit *= 2
        low = low.astype(jnp.bfloat16).reshape(requests, 2, rank2)
        ours = second.reshape(hot, rank, width)
        resident = jnp.where(
            group == 0, jnp.stack([ours, theirs], 1), jnp.stack([theirs, ours], 1)
        )
        (out,) = unpack(
            me, dest_all, count_all, earlier_token_cache, {}, None, None, pairs, context, None
        )
        small = attend(
            place, counts, request_hot_entry, low, resident, base, cos, sin, query,
            earlier_token_cache, slots, out,
        )
        small = small.reshape(replicas, pairs, TILE, width + LANES)
        smalls = lax.all_to_all(small, "replica", 0, 0, tiled=True)
        return smalls, resident_first, resident, out

    def nothing():
        return (
            jnp.zeros((replicas, pairs, TILE, width + LANES), jnp.bfloat16),
            jnp.zeros((hot, piece, rank2), jnp.bfloat16),
            jnp.zeros((hot, 2, rank, width), jnp.bfloat16),
            jnp.zeros((slots, 2, context, width), jnp.bfloat16),
        )

    smalls, resident_first, resident_second, out = lax.cond(always, serve, nothing)
    moved_cache, attended = unpack(
        me, dest_all, count_all, None, received, smalls, out, pairs, context, resident_first
    )
    moved_attention = (
        attended.reshape(slots, 2, group_size, heads, HEAD_WIDTH)
        .transpose(0, 1, 3, 2, 4)
        .reshape(slots, 2, group_size * width)
    )
    return (moved_cache, moved_attention, resident_first, resident_second)


def solution(mesh):
    in_specs = (
        P(("groups", "replica"), None, None),
        P(("groups", "replica"), None, "tensor"),
        P(("groups", "replica"), None, None, "tensor"),
        P(("groups", "replica"), None),
        P(("groups", "replica")),
        P(("groups", "replica")),
        P("groups"),
        P(None, None, "tensor"),
        P("replica", "tensor", None),
        P("replica", None, None, "tensor"),
    )
    out_specs = (
        P(("groups", "replica"), None, None, "tensor"),
        P(("groups", "replica"), None, "tensor"),
        P("groups", "tensor", None),
        P("groups", None, None, "tensor"),
    )
    return jax.shard_map(
        per_device, mesh=mesh, in_specs=in_specs, out_specs=out_specs, check_vma=False
    )
```

profile of v0, /device:TPU:0, one launch (start us, length us, event | category | flops | bytes accessed | tf_op | source)
XLA Modules:
  0.0 118.8 jit_solution(6605608697100704491)
XLA Ops:
  0.7 0.8 convert.19
  1.4 0.7 convert_bitcast_fusion
  2.2 0.8 dynamic-slice_bitcast_fusion.1
  3.1 4.1 %collective-permute-start.6 = (bf16[1168,256]{1,0:T(8,128)(2,1)S(1)}, bf16[1168,256]{1,0:T(8,128)(2,1)S(1)}, u32[]{:S(2)}, u32[]{:S(2)}) collective-permute-start(bf16[1168,256]{1,0:T(8,128)(2,1)S(1)} %pad_maximum_fusion), channel_id=1, source_target_pairs={{0,8},{4,12},{8,0},{12,4},{1,9},{5,13},{9,1},{13,5},{2,10},{6,14},... | collective-permute-start | bytes 1794056 | tf_op jit(solution)/shard_map/ppermute | solution.py:22
  7.2 1.6 %collective-permute-start.5 = (bf16[1168,256]{1,0:T(8,128)(2,1)S(1)}, bf16[1168,256]{1,0:T(8,128)(2,1)S(1)}, u32[]{:S(2)}, u32[]{:S(2)}) collective-permute-start(bf16[1168,256]{1,0:T(8,128)(2,1)S(1)} %pad_maximum_fusion), channel_id=1, source_target_pairs={{0,4},{4,0},{8,12},{12,8},{1,5},{5,1},{9,13},{13,9},{2,6},{6,2},{1... | collective-permute-start | bytes 1794056 | tf_op jit(solution)/shard_map/ppermute | solution.py:22
  8.8 0.7 compare_select_fusion
  9.5 0.7 convert.22
  10.1 1.3 %gather_fusion = s32[8]{0:T(128)S(1)} fusion(s32[2]{0:T(128)} %param.18, s32[1024]{0:T(1024)S(1)} %pad_clamp_fusion), kind=kCustom, calls=%fused_computation | custom fusion | bytes 96 | tf_op jit(solution)/shard_map/gather | solution.py:486
  11.8 1.1 reshape.117
  12.9 0.6 fusion.5.refs_0_
  13.6 4.0 %pack.1 = (bf16[6,2,128,256]{3,2,1,0:T(8,128)(2,1)}, bf16[6,2,128,256]{3,2,1,0:T(8,128)(2,1)}, bf16[6,2,128,256]{3,2,1,0:T(8,128)(2,1)}, f32[8,128]{1,0:T(8,128)}) custom-call(s32[1]{0:T(128)} %bitcast.6.me_ref.refs_0_, s32[8]{0:T(128)} %dest_ref.1, s32[8]{0:T(128)} %bitcast.40, bf16[8,2,512,256]{3,2,1,0:T(8,128)(2,1)} %cache_ref.1), custom_call_target="tpu_custom_call" | custom-call | flops 1 | bytes 1 | tf_op jit(solution)/shard_map/pack/pallas_call | solution.py:87
  17.5 1.6 %collective-permute-start.8 = (bf16[16,1152]{1,0:T(8,128)(2,1)}, bf16[16,1152]{1,0:T(8,128)(2,1)S(1)}, u32[]{:S(2)}, u32[]{:S(2)}) collective-permute-start(bf16[16,1152]{1,0:T(8,128)(2,1)} %gate.4), channel_id=1, source_target_pairs={{0,16},{16,0},{1,17},{17,1},{2,18},{18,2},{3,19},{19,3},{4,20},{20... | collective-permute-start | bytes 110600 | tf_op jit(solution)/shard_map/ppermute | solution.py:22
  19.2 4.7 %fusion = f32[8,2,2,256]{3,0,2,1:T(8,128)S(1)} fusion(bf16[8192,2,256]{2,1,0:T(2,128)(2,1)} %param.19, bf16[8,2,8192,1]{2,1,0,3:T(2,128)(2,1)S(1)} %bitcast.33), kind=kOutput, calls=%fused_computation.7 | convolution fusion | flops 134217728 | bytes 8683520 | tf_op jit(solution)/shard_map/ntd,dkc->ntkc/dot_general | solution.py:501
  24.7 0.6 reshape.118
  25.4 0.6 copy.58
  26.7 7.0 %collective-permute-done.6.refs_3_ = bf16[1168,256]{1,0:T(8,128)(2,1)S(1)} collective-permute-done((bf16[1168,256]{1,0:T(8,128)(2,1)S(1)}, bf16[1168,256]{1,0:T(8,128)(2,1)S(1)}, u32[]{:S(2)}, u32[]{:S(2)}) %collective-permute-start.6) | collective-permute-done | bytes 598048 | tf_op jit(solution)/shard_map/ppermute | solution.py:22
  34.3 0.7 pad_add_fusion
  35.0 0.7 broadcast_in_dim.20.refs_6_
  35.7 1.4 %collective-permute-start.9 = (bf16[6,2,128,256]{3,2,1,0:T(8,128)(2,1)}, bf16[6,2,128,256]{3,2,1,0:T(8,128)(2,1)}, u32[]{:S(2)}, u32[]{:S(2)}) collective-permute-start(bf16[6,2,128,256]{3,2,1,0:T(8,128)(2,1)} %get-tuple-element.102), channel_id=1, source_target_pairs={{0,4},{4,0},{8,12},{12,8},{1,5},{5,1},{9,13},{13,9},{2,6},{6,2},{1... | collective-permute-start | bytes 2359304 | tf_op jit(solution)/shard_map/ppermute | solution.py:22
  37.1 2.0 %collective-permute-start.10 = (bf16[6,2,128,256]{3,2,1,0:T(8,128)(2,1)}, bf16[6,2,128,256]{3,2,1,0:T(8,128)(2,1)}, u32[]{:S(2)}, u32[]{:S(2)}) collective-permute-start(bf16[6,2,128,256]{3,2,1,0:T(8,128)(2,1)} %get-tuple-element.103), channel_id=1, source_target_pairs={{0,8},{4,12},{8,0},{12,4},{1,9},{5,13},{9,1},{13,5},{2,10},{6,14},... | collective-permute-start | bytes 2359304 | tf_op jit(solution)/shard_map/ppermute | solution.py:22
  39.0 1.5 %collective-permute-start.11 = (bf16[6,2,128,256]{3,2,1,0:T(8,128)(2,1)}, bf16[6,2,128,256]{3,2,1,0:T(8,128)(2,1)}, u32[]{:S(2)}, u32[]{:S(2)}) collective-permute-start(bf16[6,2,128,256]{3,2,1,0:T(8,128)(2,1)} %get-tuple-element.104), channel_id=1, source_target_pairs={{0,12},{4,8},{8,4},{12,0},{1,13},{5,9},{9,5},{13,1},{2,14},{6,10},... | collective-permute-start | bytes 2359304 | tf_op jit(solution)/shard_map/ppermute | solution.py:22
  40.7 0.7 pad_maximum_fusion.2
  41.4 0.7 fusion.13
  42.0 24.9 %collective-permute-done.7 = bf16[1168,256]{1,0:T(8,128)(2,1)S(1)} collective-permute-done((bf16[1168,256]{1,0:T(8,128)(2,1)S(1)}, bf16[1168,256]{1,0:T(8,128)(2,1)S(1)}, u32[]{:S(2)}, u32[]{:S(2)}) %collective-permute-start.7) | collective-permute-done | bytes 598048 | tf_op jit(solution)/shard_map/ppermute | solution.py:22
  66.9 0.8 maximum_convert_fusion
  67.7 0.7 fusion.15
  68.9 44.2 %conditional.1 = (bf16[4,2,16,384]{3,2,1,0:T(8,128)(2,1)}, bf16[2,2048,256]{2,1,0:T(8,128)(2,1)}, bf16[8,2,512,256]{3,2,1,0:T(8,128)(2,1)}, bf16[2,2,128,256]{3,2,1,0:T(8,128)(2,1)}) conditional(s32[]{:T(128)} %bitcast.13, () %tuple.16, (s32[8]{0:T(128)}, s32[8]{0:T(128)}, s32[8,8]{1,0:T(8,128)}, bf16[16,1152]{1,0:T(8,128)(2,1)}, s32[]{:T(128)}, ...), branch_computations={%region_0.1_spmd, %region_1.3_spmd} | conditional | flops 409680 | bytes 13690051 | solution.py:571
  68.9 1.3 %bitcast_convert_fusion.other_ref = s32[2]{0:T(128)} fusion(bf16[16,1152]{1,0:T(8,128)(2,1)} %get-tuple-element.61), kind=kLoop, calls=%fused_computation.5 | loop fusion | flops 2 | bytes 12 | tf_op jit(solution)/shard_map/convert_element_type | solution.py:495
  70.2 3.2 %adapt.1 = (bf16[2,2048,256]{2,1,0:T(8,128)(2,1)}, bf16[2,128,256]{2,1,0:T(8,128)(2,1)}, bf16[2,1024,256]{2,1,0:T(8,128)(2,1)}, bf16[2,128,256]{2,1,0:T(8,128)(2,1)}, f32[32,256]{1,0:T(8,128)}) custom-call(s32[1]{0:T(128)} %get-tuple-element.59.me_ref.refs_0_, s32[2]{0:T(128)S(1)} %get-tuple-element.60.own_ref, s32[2]{0:T(128)} %bitcast_convert_fusion.other_ref, ...), custom_call_target="tpu_custom_call" | custom-call | flops 1 | bytes 1 | tf_op jit(solution)/shard_map/cond/branch_1_fun/adapt/pallas_call | solution.py:303
  73.4 0.7 slice.27
  74.1 1.6 %collective-permute-start = (f32[16,256]{1,0:T(8,128)S(1)}, f32[16,256]{1,0:T(8,128)S(1)}, u32[]{:S(2)}, u32[]{:S(2)}) collective-permute-start(f32[16,256]{1,0:T(8,128)S(1)} %slice.27), channel_id=1, source_target_pairs={{0,16},{16,0},{1,17},{17,1},{2,18},{18,2},{3,19},{19,3},{4,20},{20... | collective-permute-start | bytes 49160 | tf_op jit(solution)/shard_map/cond/branch_1_fun/ppermute | solution.py:22
  76.1 1.7 %collective-permute-done = f32[16,256]{1,0:T(8,128)S(1)} collective-permute-done((f32[16,256]{1,0:T(8,128)S(1)}, f32[16,256]{1,0:T(8,128)S(1)}, u32[]{:S(2)}, u32[]{:S(2)}) %collective-permute-start) | collective-permute-done | bytes 16416 | tf_op jit(solution)/shard_map/cond/branch_1_fun/ppermute | solution.py:22
  77.9 1.3 %slice_add_fusion.refs_1_ = f32[16,256]{1,0:T(8,128)} fusion(f32[16,256]{1,0:T(8,128)S(1)} %collective-permute-done, f32[32,256]{1,0:T(8,128)} %get-tuple-element.69), kind=kLoop, calls=%fused_computation.4 | loop fusion | flops 4096 | bytes 49152 | tf_op jit(solution)/shard_map/cond/branch_1_fun/add | solution.py:537
  79.2 3.1 %collective-permute-done.3.refs_2_ = bf16[2,128,256]{2,1,0:T(8,128)(2,1)S(1)} collective-permute-done((bf16[2,128,256]{2,1,0:T(8,128)(2,1)}, bf16[2,128,256]{2,1,0:T(8,128)(2,1)S(1)}, u32[]{:S(2)}, u32[]{:S(2)}) %collective-permute-start.3) | collective-permute-done | bytes 131104 | tf_op jit(solution)/shard_map/cond/branch_1_fun/ppermute | solution.py:22
  82.3 0.6 copy-done.5
  83.1 0.8 reduce_sum.9
  84.5 0.7 add.40
  85.2 1.9 %collective-permute-start.2 = (f32[16,256]{1,0:T(8,128)S(1)}, f32[16,256]{1,0:T(8,128)S(1)}, u32[]{:S(2)}, u32[]{:S(2)}) collective-permute-start(f32[16,256]{1,0:T(8,128)S(1)} %add.40), channel_id=1, source_target_pairs={{0,2},{1,3},{2,0},{3,1},{4,6},{5,7},{6,4},{7,5},{8,10},{9,11},{10,... | collective-permute-start | bytes 49160 | tf_op jit(solution)/shard_map/cond/branch_1_fun/ppermute | solution.py:22
  87.0 1.2 multiply_add_fusion.place_ref
  88.3 3.8 %unpack.1._ = bf16[8,2,512,256]{3,2,1,0:T(8,128)(2,1)} custom-call(s32[1]{0:T(128)} %get-tuple-element.59.me_ref.refs_0_, s32[4,8]{1,0:T(4,128)} %get-tuple-element.77.refs_1_, s32[4,8]{1,0:T(4,128)S(1)} %get-tuple-element.78.refs_2_, bf16[8,2,512,256]{3,2,1,0:T(8,128)(2,1)} %get-tuple-element.76.refs_3_.cache_ref), custom_call_target="tpu_custom_call" | custom-call | flops 1 | bytes 1 | tf_op jit(solution)/shard_map/cond/branch_1_fun/unpack/pallas_call | solution.py:255
  92.1 0.6 copy.57
  93.4 9.8 %attend.1 = bf16[8,16,384]{2,1,0:T(8,128)(2,1)} custom-call(s32[8]{0:T(128)} %multiply_add_fusion.place_ref, s32[8]{0:T(128)S(1)} %copy-done.14, s32[8]{0:T(128)S(1)} %copy-done.17, bf16[8,2,256]{2,1,0:T(2,128)(2,1)} %reshape.106.low_ref, bf16[2,2,128,256]{3,2,1,0:T(8,128)(2,1)S(1)} %copy.35.second_ref, f32[8,2,512]{2,1,0:T(2,128)S(1)} %get-tuple-element.72.base_ref, ...), custom_call_target="tpu_custom_call" | custom-call | flops 1 | bytes 1 | tf_op jit(solution)/shard_map/cond/branch_1_fun/attend/pallas_call | solution.py:408
  103.3 3.9 %all-to-all-start = ((bf16[4,2,16,384]{3,2,1,0:T(8,128)(2,1)}), bf16[4,2,16,384]{3,2,1,0:T(8,128)(2,1)}, u32[]{:S(2)}, u32[]{:S(2)}) async-start(bf16[4,2,16,384]{3,2,1,0:T(8,128)(2,1)} %bitcast.35), calls=%async_computation | async-start | bytes 196608 | tf_op jit(solution)/shard_map/cond/branch_1_fun/all_to_all | solution.py:560
  107.2 1.0 copy-done.4
  108.2 2.2 %place_half.1 = bf16[2,2048,256]{2,1,0:T(8,128)(2,1)} custom-call(s32[1]{0:T(128)} %bitcast.1.group_ref, bf16[2,1024,256]{2,1,0:T(8,128)(2,1)} %copy-done.4, bf16[2,2048,256]{2,1,0:T(8,128)(2,1)} %get-tuple-element.80._), custom_call_target="tpu_custom_call", output_to_operand_aliasing={{}: (2, {})} | custom-call | flops 1 | bytes 1 | tf_op jit(solution)/shard_map/cond/branch_1_fun/place_half/pallas_call | solution.py:330
  110.4 2.7 %all-to-all-done = bf16[4,2,16,384]{3,2,1,0:T(8,128)(2,1)} async-done(((bf16[4,2,16,384]{3,2,1,0:T(8,128)(2,1)}), bf16[4,2,16,384]{3,2,1,0:T(8,128)(2,1)}, u32[]{:S(2)}, u32[]{:S(2)}) %all-to-all-start) | async-done | bytes 98336 | tf_op jit(solution)/shard_map/cond/branch_1_fun/all_to_all | solution.py:560
  113.1 4.2 %unpack_tail.1 = (bf16[8,2,512,256]{3,2,1,0:T(8,128)(2,1)}, bf16[8,16,256]{2,1,0:T(8,128)(2,1)}) custom-call(s32[1]{0:T(128)} %bitcast.6.me_ref.refs_0_, s32[4,8]{1,0:T(4,128)} %get-tuple-element.174.refs_1_, s32[4,8]{1,0:T(4,128)S(1)} %get-tuple-element.173.refs_2_, ...), custom_call_target="tpu_custom_call", output_to_operand_aliasing={{0}: (7, {})} | custom-call | flops 1 | bytes 1 | tf_op jit(solution)/shard_map/unpack_tail/pallas_call | solution.py:255
  117.3 1.5 %reshape.122 = bf16[8,2,2048]{2,1,0:T(2,128)(2,1)} reshape(bf16[8,2,2,8,128]{4,3,2,1,0:T(8,128)(2,1)} %bitcast.39) | data formatting | bytes 131072 | tf_op jit(solution)/shard_map/reshape | solution.py:578
  (81 shorter events, 5.3 us)
Async XLA Ops:
  0.6 2.4 %copy-start = (bf16[1,2048,256]{2,1,0:T(8,128)(2,1)S(1)}, bf16[1,2048,256]{2,1,0:T(8,128)(2,1)}, u32[]{:S(2)}) copy-start(bf16[1,2048,256]{2,1,0:T(8,128)(2,1)} %param.20) | copy-start | bytes 3145732
  0.6 18.5 %copy-start.2 = (bf16[8,2,8192]{2,1,0:T(2,128)(2,1)S(1)}, bf16[8,2,8192]{2,1,0:T(2,128)(2,1)}, u32[]{:S(2)}) copy-start(bf16[8,2,8192]{2,1,0:T(2,128)(2,1)} %param.12) | copy-start | bytes 786436
  1.4 1.7 %copy-start.15 = (bf16[1,8]{1,0:T(2,128)(2,1)}, bf16[1,8]{1,0:T(2,128)(2,1)S(1)}, u32[]{:S(2)}) copy-start(bf16[1,8]{1,0:T(2,128)(2,1)S(1)} %convert.19) | copy-start | bytes 52
  2.1 1.0 copy-start.16
  3.1 30.5 %collective-permute-start.6 = (bf16[1168,256]{1,0:T(8,128)(2,1)S(1)}, bf16[1168,256]{1,0:T(8,128)(2,1)S(1)}, u32[]{:S(2)}, u32[]{:S(2)}) collective-permute-start(bf16[1168,256]{1,0:T(8,128)(2,1)S(1)} %pad_maximum_fusion), channel_id=1, source_target_pairs={{0,8},{4,12},{8,0},{12,4},{1,9},{5,13},{9,1},{13,5},{2,10},{6,14},... | collective-permute-start | bytes 1794056 | tf_op jit(solution)/shard_map/ppermute | solution.py:22
  7.2 27.8 %collective-permute-start.5 = (bf16[1168,256]{1,0:T(8,128)(2,1)S(1)}, bf16[1168,256]{1,0:T(8,128)(2,1)S(1)}, u32[]{:S(2)}, u32[]{:S(2)}) collective-permute-start(bf16[1168,256]{1,0:T(8,128)(2,1)S(1)} %pad_maximum_fusion), channel_id=1, source_target_pairs={{0,4},{4,0},{8,12},{12,8},{1,5},{5,1},{9,13},{13,9},{2,6},{6,2},{1... | collective-permute-start | bytes 1794056 | tf_op jit(solution)/shard_map/ppermute | solution.py:22
  17.5 8.5 %collective-permute-start.8 = (bf16[16,1152]{1,0:T(8,128)(2,1)}, bf16[16,1152]{1,0:T(8,128)(2,1)S(1)}, u32[]{:S(2)}, u32[]{:S(2)}) collective-permute-start(bf16[16,1152]{1,0:T(8,128)(2,1)} %gate.4), channel_id=1, source_target_pairs={{0,16},{16,0},{1,17},{17,1},{2,18},{18,2},{3,19},{19,3},{4,20},{20... | collective-permute-start | bytes 110600 | tf_op jit(solution)/shard_map/ppermute | solution.py:22
  19.2 4.7 %copy-start.13 = (s32[1,8]{1,0:T(1,128)S(1)}, s32[1,8]{1,0:T(1,128)}, u32[]{:S(2)}) copy-start(s32[1,8]{1,0:T(1,128)} %param.15) | copy-start | bytes 100
  19.2 6.2 %copy-start.9 = (bf16[8,2,2048]{2,1,0:T(2,128)(2,1)S(1)}, bf16[8,2,2048]{2,1,0:T(2,128)(2,1)}, u32[]{:S(2)}) copy-start(bf16[8,2,2048]{2,1,0:T(2,128)(2,1)} %param.13) | copy-start | bytes 196612
  23.8 17.5 %copy-start.12 = (s32[8]{0:T(128)S(1)}, s32[8]{0:T(128)}, u32[]{:S(2)}) copy-start(s32[8]{0:T(128)} %dest_ref.1) | copy-start | bytes 100
  23.9 45.0 %copy-start.1 = (s32[2]{0:T(128)S(1)}, s32[2]{0:T(128)}, u32[]{:S(2)}) copy-start(s32[2]{0:T(128)} %param.18) | copy-start | bytes 28
  24.6 15.9 %copy-start.18 = (f32[64]{0:T(128)S(1)}, f32[64]{0:T(128)}, u32[]{:S(2)}) copy-start(f32[64]{0:T(128)} %negate_power_fusion) | copy-start | bytes 772
  26.1 0.6 copy-start.10
  33.6 33.3 %collective-permute-start.7 = (bf16[1168,256]{1,0:T(8,128)(2,1)S(1)}, bf16[1168,256]{1,0:T(8,128)(2,1)S(1)}, u32[]{:S(2)}, u32[]{:S(2)}) collective-permute-start(bf16[1168,256]{1,0:T(8,128)(2,1)S(1)} %collective-permute-done.6.refs_3_), channel_id=1, source_target_pairs={{0,4},{4,0},{8,12},{12,8},{1,5},{5,1},{9,13},{13,9},{2,6},{6,2},{1... | collective-permute-start | bytes 1794056 | tf_op jit(solution)/shard_map/ppermute | solution.py:22
  35.7 77.4 %collective-permute-start.9 = (bf16[6,2,128,256]{3,2,1,0:T(8,128)(2,1)}, bf16[6,2,128,256]{3,2,1,0:T(8,128)(2,1)}, u32[]{:S(2)}, u32[]{:S(2)}) collective-permute-start(bf16[6,2,128,256]{3,2,1,0:T(8,128)(2,1)} %get-tuple-element.102), channel_id=1, source_target_pairs={{0,4},{4,0},{8,12},{12,8},{1,5},{5,1},{9,13},{13,9},{2,6},{6,2},{1... | collective-permute-start | bytes 2359304 | tf_op jit(solution)/shard_map/ppermute | solution.py:22
  37.1 76.0 %collective-permute-start.10 = (bf16[6,2,128,256]{3,2,1,0:T(8,128)(2,1)}, bf16[6,2,128,256]{3,2,1,0:T(8,128)(2,1)}, u32[]{:S(2)}, u32[]{:S(2)}) collective-permute-start(bf16[6,2,128,256]{3,2,1,0:T(8,128)(2,1)} %get-tuple-element.103), channel_id=1, source_target_pairs={{0,8},{4,12},{8,0},{12,4},{1,9},{5,13},{9,1},{13,5},{2,10},{6,14},... | collective-permute-start | bytes 2359304 | tf_op jit(solution)/shard_map/ppermute | solution.py:22
  39.0 74.0 %collective-permute-start.11 = (bf16[6,2,128,256]{3,2,1,0:T(8,128)(2,1)}, bf16[6,2,128,256]{3,2,1,0:T(8,128)(2,1)}, u32[]{:S(2)}, u32[]{:S(2)}) collective-permute-start(bf16[6,2,128,256]{3,2,1,0:T(8,128)(2,1)} %get-tuple-element.104), channel_id=1, source_target_pairs={{0,12},{4,8},{8,4},{12,0},{1,13},{5,9},{9,5},{13,1},{2,14},{6,10},... | collective-permute-start | bytes 2359304 | tf_op jit(solution)/shard_map/ppermute | solution.py:22
  74.1 3.7 %collective-permute-start = (f32[16,256]{1,0:T(8,128)S(1)}, f32[16,256]{1,0:T(8,128)S(1)}, u32[]{:S(2)}, u32[]{:S(2)}) collective-permute-start(f32[16,256]{1,0:T(8,128)S(1)} %slice.27), channel_id=1, source_target_pairs={{0,16},{16,0},{1,17},{17,1},{2,18},{18,2},{3,19},{19,3},{4,20},{20... | collective-permute-start | bytes 49160 | tf_op jit(solution)/shard_map/cond/branch_1_fun/ppermute | solution.py:22
  75.7 6.6 %collective-permute-start.3 = (bf16[2,128,256]{2,1,0:T(8,128)(2,1)}, bf16[2,128,256]{2,1,0:T(8,128)(2,1)S(1)}, u32[]{:S(2)}, u32[]{:S(2)}) collective-permute-start(bf16[2,128,256]{2,1,0:T(8,128)(2,1)} %get-tuple-element.71), channel_id=1, source_target_pairs={{0,16},{16,0},{1,17},{17,1},{2,18},{18,2},{3,19},{19,3},{4,20},{20... | collective-permute-start | bytes 393224 | tf_op jit(solution)/shard_map/cond/branch_1_fun/ppermute | solution.py:22
  82.3 0.6 copy-start.5
  82.9 24.2 %collective-permute-start.4 = (bf16[2,1024,256]{2,1,0:T(8,128)(2,1)}, bf16[2,1024,256]{2,1,0:T(8,128)(2,1)S(1)}, u32[]{:S(2)}, u32[]{:S(2)}) collective-permute-start(bf16[2,1024,256]{2,1,0:T(8,128)(2,1)} %gate.3), channel_id=1, source_target_pairs={{0,16},{16,0},{1,17},{17,1},{2,18},{18,2},{3,19},{19,3},{4,20},{20... | collective-permute-start | bytes 3145736 | tf_op jit(solution)/shard_map/cond/branch_1_fun/ppermute | solution.py:22
  83.1 1.4 %collective-permute-start.1 = (f32[16,256]{1,0:T(8,128)}, f32[16,256]{1,0:T(8,128)S(1)}, u32[]{:S(2)}, u32[]{:S(2)}) collective-permute-start(f32[16,256]{1,0:T(8,128)} %slice_add_fusion.refs_1_), channel_id=1, source_target_pairs={{0,1},{1,0},{2,3},{3,2},{4,5},{5,4},{6,7},{7,6},{8,9},{9,8},{10,11... | collective-permute-start | bytes 49160 | tf_op jit(solution)/shard_map/cond/branch_1_fun/ppermute | solution.py:22
  85.2 7.5 %collective-permute-start.2 = (f32[16,256]{1,0:T(8,128)S(1)}, f32[16,256]{1,0:T(8,128)S(1)}, u32[]{:S(2)}, u32[]{:S(2)}) collective-permute-start(f32[16,256]{1,0:T(8,128)S(1)} %add.40), channel_id=1, source_target_pairs={{0,2},{1,3},{2,0},{3,1},{4,6},{5,7},{6,4},{7,5},{8,10},{9,11},{10,... | collective-permute-start | bytes 49160 | tf_op jit(solution)/shard_map/cond/branch_1_fun/ppermute | solution.py:22
  88.2 3.8 %copy-start.7 = (bf16[8,2,2,8,128]{4,3,1,0,2:T(8,128)(2,1)S(1)}, bf16[8,2,2,8,128]{4,3,1,0,2:T(8,128)(2,1)}, u32[]{:S(2)}) copy-start(bf16[8,2,2,8,128]{4,3,1,0,2:T(8,128)(2,1)} %get-tuple-element.154) | copy-start | bytes 196612 | tf_op jit(solution)/shard_map/cond
  88.2 5.1 %copy-start.6 = (bf16[2,128,256]{2,1,0:T(8,128)(2,1)S(1)}, bf16[2,128,256]{2,1,0:T(8,128)(2,1)}, u32[]{:S(2)}) copy-start(bf16[2,128,256]{2,1,0:T(8,128)(2,1)} %copy-done.5) | copy-start | bytes 393220 | tf_op jit(solution)/shard_map/cond
  88.2 5.1 %copy-start.8 = (bf16[2,128,256]{2,1,0:T(8,128)(2,1)S(1)}, bf16[2,128,256]{2,1,0:T(8,128)(2,1)}, u32[]{:S(2)}) copy-start(bf16[2,128,256]{2,1,0:T(8,128)(2,1)} %get-tuple-element.70) | copy-start | bytes 393220 | tf_op jit(solution)/shard_map/cond
  88.2 5.2 %copy-start.11 = (f32[8,2,128]{2,1,0:T(2,128)S(1)}, f32[8,2,128]{2,1,0:T(2,128)}, u32[]{:S(2)}) copy-start(f32[8,2,128]{2,1,0:T(2,128)} %get-tuple-element.74.sin_ref) | copy-start | bytes 24580 | tf_op jit(solution)/shard_map/cond
  88.2 5.2 %copy-start.14 = (s32[8]{0:T(128)S(1)}, s32[8]{0:T(128)}, u32[]{:S(2)}) copy-start(s32[8]{0:T(128)} %get-tuple-element.57.count_ref) | copy-start | bytes 100 | tf_op jit(solution)/shard_map/cond
  88.2 5.2 %copy-start.17 = (s32[8]{0:T(128)S(1)}, s32[8]{0:T(128)}, u32[]{:S(2)}) copy-start(s32[8]{0:T(128)} %get-tuple-element.58.hot_ref) | copy-start | bytes 100 | tf_op jit(solution)/shard_map/cond
  93.4 9.9 %copy-start.3 = (bf16[2,2,128,256]{3,2,1,0:T(8,128)(2,1)}, bf16[2,2,128,256]{3,2,1,0:T(8,128)(2,1)S(1)}, u32[]{:S(2)}) copy-start(bf16[2,2,128,256]{3,2,1,0:T(8,128)(2,1)S(1)} %copy.35.second_ref) | copy-start | bytes 786436 | tf_op jit(solution)/shard_map/cond
  103.3 9.8 %all-to-all-start = ((bf16[4,2,16,384]{3,2,1,0:T(8,128)(2,1)}), bf16[4,2,16,384]{3,2,1,0:T(8,128)(2,1)}, u32[]{:S(2)}, u32[]{:S(2)}) async-start(bf16[4,2,16,384]{3,2,1,0:T(8,128)(2,1)} %bitcast.35), calls=%async_computation | async-start | bytes 196608 | tf_op jit(solution)/shard_map/cond/branch_1_fun/all_to_all | solution.py:560
  107.2 1.0 copy-start.4
where the time goes:
time: 120 us; the launch traced here: 119 us
  waiting for transfers between devices  40 us (33%)
  Pallas kernels  27.2 us (23%)
  starting transfers between devices  20.7 us (17%)
  other arithmetic  12.7 us (11%)
  local copies, waits for them, and re-layouts  12.5 us (10%)
  matrix products  4.65 us (4%)
    ppermute x12, waiting for transfers between devices, exchange(): return lax.ppermute(values, axis, [(i, i ^ mask) for i in range(size)])  37.3 us
    ppermute x12, starting transfers between devices, exchange(): return lax.ppermute(values, axis, [(i, i ^ mask) for i in range(size)])  16.8 us
    pallas_call x1, Pallas kernels, attend(): pl.pallas_call(attend_kernel, out_shape=jax.ShapeDtypeStruct((slots, TILE...  9.84 us
    pallas_call x2, Pallas kernels, unpack(): pl.pallas_call(functools.partial(unpack_kernel, layout, own, fill, tail,...  8 us
    dot_general x1, matrix products, per_device(): jnp.einsum('ntd,dkc->ntkc', hidden, base_key_value_weight, preferred_elem...  4.65 us
    pallas_call x1, Pallas kernels, pack(): pl.pallas_call(functools.partial(pack_kernel, layout, live), out_shape=[j...  3.97 us
    all_to_all x1, starting transfers between devices, serve(): smalls = lax.all_to_all(small, 'replica', 0, 0, tiled=True)  3.91 us
    pallas_call x1, Pallas kernels, adapt(): pl.pallas_call(functools.partial(adapt_kernel, half, extra, len(pieces)),...  3.2 us
  transfers between devices with their start and end apart: 13, of which 6 were waited for; matrix products, arithmetic and copies ran while one was open for 20% of the time, Pallas kernels for 19%

commit v1 on v0

--- a/solution.py
+++ b/solution.py
@@ -1,4 +1,5 @@
 import functools
+import math
 
 import jax
 import jax.numpy as jnp
@@ -116,8 +117,7 @@
     if tail:
         small_ref = refs[at]
         at += 1
-    if not fill:
-        at += 2
+    at += 1 if fill else 2
     out_ref = refs[at]
     at += 1
     if tail:
@@ -145,23 +145,36 @@
         return pltpu.make_async_copy(source, target, sems.at[used - 1])
 
     slot_info = []
+    used_patterns = {of for of, _, _ in layout} | ({0} if own else set())
     for pattern in range(replicas):
+        if not (fill or tail or pattern in used_patterns):
+            continue
         source_replica = me ^ pattern
         arrived = jnp.int32(0)
-        offset = jnp.int32(0)
         lengths_of = [jnp.int32(-1)] * pairs
+        which = [jnp.int32(0)] * pairs
         for r in range(requests):
             mine = dest_ref[pattern, r] == me
             blocks = count_ref[pattern, r]
-            slot = source_replica * pairs + jnp.minimum(arrived, pairs - 1)
+            for k in range(pairs):
+                this = mine & (arrived == k)
+                lengths_of[k] = jnp.where(this, blocks, lengths_of[k])
+                which[k] = jnp.where(this, r, which[k])
+            arrived = arrived + jnp.where(mine, 1, 0)
+        offset = jnp.int32(0)
+        for k in range(pairs):
+            blocks = lengths_of[k]
+            slot = source_replica * pairs + k
             for b in range(live):
                 place = pl.ds(b * BLOCK, BLOCK)
                 target = out_ref.at[slot, :, place, :]
-                valid = mine & (b < blocks)
+                valid = b < blocks
                 if pattern == 0 and own:
-                    index = r * live + b
+                    index = k * live + b
                     inward = pltpu.make_async_copy(
-                        cache_ref.at[r, :, place, :], own_stage.at[index], own_sems.at[index]
+                        cache_ref.at[which[k], :, place, :],
+                        own_stage.at[index],
+                        own_sems.at[index],
                     )
                     moves.append((valid, inward, [(valid, copy_to(own_stage.at[index], target))]))
                 for (of, first, amount), received_ref in zip(layout, received):
@@ -170,13 +183,8 @@
                         source = received_ref.at[jnp.clip(here, 0, amount - 1)]
                         inside = valid & (here >= 0) & (here < amount)
                         copies.append((inside, copy_to(source, target)))
-            lengths_of = [
-                jnp.where(mine & (arrived == k), blocks, lengths_of[k]) for k in range(pairs)
-            ]
-            arrived = arrived + jnp.where(mine, 1, 0)
-            offset = offset + jnp.where(mine, blocks, 0)
-        for k in range(pairs):
-            slot_info.append((pattern, k, source_replica * pairs + k, lengths_of[k]))
+            offset = offset + jnp.maximum(blocks, 0)
+            slot_info.append((pattern, k, slot, blocks))
     if fill:
         for pattern, k, slot, blocks in slot_info:
             for b in range(live + 1):
@@ -187,20 +195,16 @@
     for condition, copy in copies:
         pl.when(condition)(copy.start)
     if tail:
-        rows = lax.broadcasted_iota(jnp.int32, (TILE, LANES), 0)
-        heads = width // LANES
+        columns = att_ref.shape[2]
         for index, (pattern, k, slot, blocks) in enumerate(slot_info):
             small = small_ref[me ^ pattern, k]
             filled = blocks >= 0
-            att_ref[slot] = jnp.where(filled, small[:, :width], jnp.zeros((), small.dtype))
-            fresh = small[:, width:].astype(jnp.float32)
+            att_ref[slot] = jnp.where(filled, small[:, :columns], jnp.zeros((), small.dtype))
+            fresh = small[:, columns:].astype(jnp.float32)
             for kv in range(2):
-                for head in range(heads):
-                    at_row = 2 * (kv * heads + head)
-                    moved = pltpu.roll(fresh, (TILE - at_row) % TILE, 0)
-                    stage_ref[index, kv, :, pl.ds(head * LANES, LANES)] = jnp.where(
-                        rows < 2, moved, 0.0
-                    ).astype(jnp.bfloat16)
+                rows = fresh[:, kv * width : (kv + 1) * width]
+                rows = jnp.concatenate([rows, jnp.zeros((TILE - 2, width), jnp.float32)], 0)
+                stage_ref[index, kv] = rows.astype(jnp.bfloat16)
             start = pl.multiple_of(jnp.maximum(blocks, 0) * BLOCK, BLOCK)
             copy = copy_to(stage_ref.at[index], out_ref.at[slot, :, pl.ds(start, TILE), :])
             pl.when(filled)(copy.start)
@@ -218,7 +222,7 @@
     replicas, requests = dest_all.shape
     own, fill, tail = cache is not None, out is None, smalls is not None
     layout = tuple(sorted(received))
-    like = cache if own else received[layout[0]]
+    like = cache if own else out
     dtype, width = like.dtype, like.shape[-1]
     live = context // BLOCK - 1
     slots = replicas * pairs
@@ -235,21 +239,23 @@
     aliases = {}
     if not fill:
         aliases = {len(args): 0}
-        args += [out, after]
-        specs += [HBM] * 2
+        args.append(out)
+        specs.append(HBM)
+    args.append(after)
+    specs.append(HBM)
     out_shape = [jax.ShapeDtypeStruct((slots, 2, context, width), dtype)]
     out_specs = [HBM]
-    amount = (len(layout) + (1 if own else 0)) * requests * live
+    amount = (len(layout) + (1 if own else 0)) * pairs * live
     scratch = []
     if own:
-        scratch.append(pltpu.VMEM((requests * live, 2, BLOCK, width), dtype))
-        scratch.append(pltpu.SemaphoreType.DMA((requests * live,)))
+        scratch.append(pltpu.VMEM((pairs * live, 2, BLOCK, width), dtype))
+        scratch.append(pltpu.SemaphoreType.DMA((pairs * live,)))
     if fill:
         amount += slots * (live + 1)
         scratch.append(pltpu.VMEM((2, BLOCK, width), dtype))
     if tail:
         amount += slots
-        out_shape.append(jax.ShapeDtypeStruct((slots, TILE, width), dtype))
+        out_shape.append(jax.ShapeDtypeStruct((slots, 2, smalls.shape[3] - 2 * width), dtype))
         out_specs.append(VMEM)
         scratch.append(pltpu.VMEM((slots, 2, TILE, width), dtype))
     return pl.pallas_call(
@@ -261,13 +267,15 @@
         input_output_aliases=aliases,
         compiler_params=pltpu.CompilerParams(vmem_limit_bytes=60 << 20),
         cost_estimate=CHEAP,
-        name="unpack_tail" if tail else "unpack",
+        name="unpack",
     )(*args)
 
 
 def adapt_kernel(half, extra, amount, me_ref, own_ref, other_ref, group_ref, ids_ref, tokens_ref, *refs):
     pieces = refs[:amount]
-    first_ref, second_ref, first_send_ref, second_send_ref, product_ref, sems = refs[amount + 1 :]
+    first_ref, second_ref, first_send_ref, second_send_ref, own_product_ref, product_ref, sems = (
+        refs[amount + 1 :]
+    )
     me, group = me_ref[0], group_ref[0]
     copies = []
 
@@ -279,19 +287,21 @@
             other = (other_ref[h] ^ me) == mask
             add(other, piece.at[pl.ds(half, extra), :], second_send_ref.at[h])
             add(other, piece.at[pl.ds(0, half), :], first_send_ref.at[h])
-            mine = (own_ref[h] ^ me) == mask
-            add(mine, piece.at[pl.ds(half, extra), :], second_ref.at[h])
+            ours = (own_ref[h] ^ me) == mask
+            add(ours, piece.at[pl.ds(half, extra), :], second_ref.at[h])
             start = pl.multiple_of(group * half, half)
-            add(mine, piece.at[pl.ds(0, half), :], first_ref.at[h, pl.ds(start, half), :])
+            add(ours, piece.at[pl.ds(0, half), :], first_ref.at[h, pl.ds(start, half), :])
     for condition, copy in copies:
         pl.when(condition)(copy.start)
-    total = jnp.zeros(product_ref.shape, jnp.float32)
+    mine = product_ref.shape[0]
+    total = jnp.zeros((2 * mine, product_ref.shape[1]), jnp.float32)
     for mask, piece in enumerate(pieces):
         product = jnp.dot(
             tokens_ref[...], piece[pl.ds(0, half), :], preferred_element_type=jnp.float32
         )
         total = total + jnp.where(ids_ref[...] == (me ^ mask), product, 0.0)
-    product_ref[...] = total
+    own_product_ref[...] = total[:mine]
+    product_ref[...] = total[mine:]
     for condition, copy in copies:
         pl.when(condition)(copy.wait)
 
@@ -307,10 +317,10 @@
             jax.ShapeDtypeStruct((hot, extra, rank2), dtype),
             jax.ShapeDtypeStruct((hot, half, rank2), dtype),
             jax.ShapeDtypeStruct((hot, extra, rank2), dtype),
-            jax.ShapeDtypeStruct((tokens.shape[0], rank2), jnp.float32),
-        ],
+        ]
+        + [jax.ShapeDtypeStruct((tokens.shape[0] // 2, rank2), jnp.float32)] * 2,
         in_specs=[SMEM] * 4 + [VMEM] * (2 + len(pieces)) + [HBM],
-        out_specs=[HBM] * 4 + [VMEM],
+        out_specs=[HBM] * 4 + [VMEM] * 2,
         scratch_shapes=[pltpu.SemaphoreType.DMA((4 * hot * len(pieces),))],
         compiler_params=pltpu.CompilerParams(vmem_limit_bytes=60 << 20),
         cost_estimate=CHEAP,
@@ -318,7 +328,7 @@
     )(me, placement, other_placement, group, ids, tokens, *pieces, after)
 
 
-def place_kernel(group_ref, received_ref, _, out_ref, sem):
+def place_kernel(group_ref, received_ref, _, after_ref, out_ref, sem):
     half = received_ref.shape[1]
     start = pl.multiple_of((1 - group_ref[0]) * half, half)
     copy = pltpu.make_async_copy(received_ref, out_ref.at[:, pl.ds(start, half), :], sem)
@@ -326,106 +336,123 @@
     copy.wait()
 
 
-def place_half(group, received, out):
+def place_half(group, received, out, after):
     return pl.pallas_call(
         place_kernel,
         out_shape=jax.ShapeDtypeStruct(out.shape, out.dtype),
-        in_specs=[SMEM, VMEM, HBM],
+        in_specs=[SMEM, VMEM, HBM, HBM],
         out_specs=HBM,
         scratch_shapes=[pltpu.SemaphoreType.DMA],
         compiler_params=pltpu.CompilerParams(vmem_limit_bytes=60 << 20),
         input_output_aliases={2: 0},
         cost_estimate=CHEAP,
         name="place_half",
-    )(group, received, out)
+    )(group, received, out, after)
 
 
 def attend_kernel(
-    place_ref, count_ref, hot_ref, low_ref, second_ref, base_ref, cos_ref, sin_ref, query_ref,
-    cache_ref, _, out_ref,
+    place_ref, count_ref, hot_ref, group_ref, low_ref, low_other_ref, ours_ref, theirs_ref, base_ref,
+    cos_ref, sin_ref, query_ref, cache_ref, out_ref, second_ref,
 ):
-    r = pl.program_id(0)
-    start = count_ref[r] * BLOCK
-    entry = hot_ref[r]
-    rank = second_ref.shape[2]
-    width = cache_ref.shape[3]
-    context = cache_ref.shape[2]
-    heads = width // LANES
-    low = low_ref[0]
-    base = base_ref[0]
-    delta_key = jnp.dot(low[:, :rank], second_ref[entry, 0], preferred_element_type=jnp.float32)
-    delta_value = jnp.dot(low[:, rank:], second_ref[entry, 1], preferred_element_type=jnp.float32)
-    key_pre = base[:, :width] + delta_key
-    new_value = (base[:, width:] + delta_value).astype(jnp.bfloat16)
-    columns = lax.broadcasted_iota(jnp.int32, (TILE, context), 1)
-    second_token = lax.broadcasted_iota(jnp.int32, (TILE, 1), 0) >= TILE // 2
-    fresh_keys, fresh_values = [], []
-    for head in range(heads):
-        lanes = slice(head * LANES, (head + 1) * LANES)
-        k = key_pre[:, lanes]
-        swapped = pltpu.roll(k, LANES // 2, 1)
-        new_key = (k * cos_ref[0] + swapped * sin_ref[0]).astype(jnp.bfloat16).astype(jnp.float32)
-        value_rows = new_value[:, lanes].astype(jnp.float32)
-        fresh_keys.append(new_key)
-        fresh_values.append(value_rows)
-        q = query_ref[0, head]
-        qf = q.astype(jnp.float32)
-        scale = HEAD_WIDTH ** (-0.5)
-        scores = lax.dot_general(
-            q, cache_ref[0, 0, :, lanes], (((1,), (1,)), ((), ())),
-            preferred_element_type=jnp.float32,
-        ) * scale
-        scores = jnp.where(columns < start, scores, -1e30)
-        s0 = jnp.sum(qf * new_key[0:1], -1, keepdims=True) * scale
-        s1 = jnp.sum(qf * new_key[1:2], -1, keepdims=True) * scale
-        s1 = jnp.where(second_token, s1, -1e30)
-        top = jnp.maximum(jnp.max(scores, -1, keepdims=True), jnp.maximum(s0, s1))
-        weights = jnp.exp(scores - top)
-        w0 = jnp.exp(s0 - top)
-        w1 = jnp.exp(s1 - top)
-        total = jnp.sum(weights, -1, keepdims=True) + w0 + w1
-        probs = (weights / total).astype(jnp.bfloat16)
-        p0 = (w0 / total).astype(jnp.bfloat16).astype(jnp.float32)
-        p1 = (w1 / total).astype(jnp.bfloat16).astype(jnp.float32)
-        attended = jnp.dot(
-            probs, cache_ref[0, 1, :, lanes], preferred_element_type=jnp.float32
-        )
-        attended = attended + p0 * value_rows[0:1] + p1 * value_rows[1:2]
-        out_ref[0, :, lanes] = attended.astype(jnp.bfloat16)
-    fresh = fresh_keys + fresh_values
-    if 2 * len(fresh) < TILE:
-        fresh.append(jnp.zeros((TILE - 2 * len(fresh), LANES), jnp.float32))
-    out_ref[0, :, width:] = jnp.concatenate(fresh, 0).astype(jnp.bfloat16)
-
-
-def attend(place, counts, hot, low, second, base, cos, sin, query, cache, slots, after):
+    step = cache_ref.shape[0]
+    second_ref[group_ref[0]] = ours_ref[...]
+    second_ref[1 - group_ref[0]] = theirs_ref[...]
+    lows = (low_ref[...] + low_other_ref[...]).astype(jnp.bfloat16)
+    for i in range(step):
+        r = pl.program_id(0) * step + i
+        start = count_ref[r] * BLOCK
+        entry = hot_ref[r]
+        rank = second_ref.shape[2]
+        width = cache_ref.shape[3]
+        context = cache_ref.shape[2]
+        heads = width // LANES
+        low = lows[2 * i : 2 * i + 2]
+        base = base_ref[i]
+        delta_key = jnp.dot(low[:, :rank], second_ref[0, entry], preferred_element_type=jnp.float32)
+        delta_value = jnp.dot(low[:, rank:], second_ref[1, entry], preferred_element_type=jnp.float32)
+        key_pre = base[:, :width] + delta_key
+        new_value = (base[:, width:] + delta_value).astype(jnp.bfloat16)
+        columns = lax.broadcasted_iota(jnp.int32, (TILE, context), 1)
+        second_token = lax.broadcasted_iota(jnp.int32, (TILE, 1), 0) >= TILE // 2
+        fresh_keys, fresh_values = [], []
+        for head in range(heads):
+            lanes = slice(head * LANES, (head + 1) * LANES)
+            k = key_pre[:, lanes]
+            swapped = pltpu.roll(k, LANES // 2, 1)
+            new_key = (k * cos_ref[i] + swapped * sin_ref[i]).astype(jnp.bfloat16).astype(jnp.float32)
+            value_rows = new_value[:, lanes].astype(jnp.float32)
+            fresh_keys.append(new_key)
+            fresh_values.append(value_rows)
+            q = query_ref[i, head]
+            qf = q.astype(jnp.float32)
+            scale = HEAD_WIDTH ** (-0.5)
+            scores = lax.dot_general(
+                q, cache_ref[i, 0, :, lanes], (((1,), (1,)), ((), ())),
+                preferred_element_type=jnp.float32,
+            ) * scale
+            scores = jnp.where(columns < start, scores, -1e30)
+            s0 = jnp.sum(qf * new_key[0:1], -1, keepdims=True) * scale
+            s1 = jnp.sum(qf * new_key[1:2], -1, keepdims=True) * scale
+            s1 = jnp.where(second_token, s1, -1e30)
+            top = jnp.maximum(jnp.max(scores, -1, keepdims=True), jnp.maximum(s0, s1))
+            weights = jnp.exp(scores - top)
+            w0 = jnp.exp(s0 - top)
+            w1 = jnp.exp(s1 - top)
+            total = jnp.sum(weights, -1, keepdims=True) + w0 + w1
+            probs = (weights / total).astype(jnp.bfloat16)
+            p0 = (w0 / total).astype(jnp.bfloat16).astype(jnp.float32)
+            p1 = (w1 / total).astype(jnp.bfloat16).astype(jnp.float32)
+            attended = jnp.dot(
+                probs, cache_ref[i, 1, :, lanes], preferred_element_type=jnp.float32
+            )
+            attended = attended + p0 * value_rows[0:1] + p1 * value_rows[1:2]
+            shared = TILE // 2
+            for j in range(shared):
+                both_tokens = jnp.concatenate(
+                    [attended[j : j + 1], attended[shared + j : shared + j + 1]], 0
+                )
+                columns_to = pl.ds((head * shared + j) * LANES, LANES)
+                out_ref[place_ref[r], :, columns_to] = both_tokens.astype(jnp.bfloat16)
+        fresh = jnp.concatenate(fresh_keys + fresh_values, 1)
+        out_ref[place_ref[r], :, shared * width :] = fresh.astype(jnp.bfloat16)
+
+
+def attend(
+    place, counts, hot, group, lows, ours, theirs, base, cos, sin, query, cache, slots
+):
     requests, _, context, width = cache.shape
     heads = width // LANES
 
+    step = math.gcd(requests, 4)
+
     def by_request(shape):
-        return pl.BlockSpec((1,) + shape, lambda r, p, c, h: (r,) + (0,) * len(shape))
+        return pl.BlockSpec((step,) + shape, lambda r, *_: (r,) + (0,) * len(shape))
 
     return pl.pallas_call(
         attend_kernel,
-        out_shape=jax.ShapeDtypeStruct((slots, TILE, width + LANES), cache.dtype),
+        out_shape=jax.ShapeDtypeStruct((slots, 2, (TILE // 2 + 2) * width), cache.dtype),
         grid_spec=pltpu.PrefetchScalarGridSpec(
-            num_scalar_prefetch=3,
-            grid=(requests,),
+            num_scalar_prefetch=4,
+            grid=(requests // step,),
             in_specs=[
-                by_request((2, low.shape[2])),
-                pl.BlockSpec(second.shape, lambda r, p, c, h: (0, 0, 0, 0)),
+                pl.BlockSpec((2 * step, lows[0].shape[1]), lambda r, *_: (r, 0)),
+                pl.BlockSpec((2 * step, lows[0].shape[1]), lambda r, *_: (r, 0)),
+                pl.BlockSpec(ours.shape, lambda r, *_: (0, 0, 0)),
+                pl.BlockSpec(ours.shape, lambda r, *_: (0, 0, 0)),
                 by_request((2, 2 * width)),
                 by_request((2, LANES)),
                 by_request((2, LANES)),
                 by_request((heads, TILE, LANES)),
                 by_request((2, context, width)),
-                HBM,
             ],
-            out_specs=pl.BlockSpec((1, TILE, width + LANES), lambda r, p, c, h: (p[r], 0, 0)),
+            out_specs=pl.BlockSpec(
+                (slots, 2, (TILE // 2 + 2) * width), lambda r, *_: (0, 0, 0)
+            ),
+            scratch_shapes=[pltpu.VMEM((2,) + ours.shape, cache.dtype)],
         ),
         cost_estimate=CHEAP,
         name="attend",
-    )(place, counts, hot, low, second, base, cos, sin, query, cache, after)
+    )(place, counts, hot, group, *lows, ours, theirs, base, cos, sin, query, cache)
 
 
 def per_device(
@@ -502,7 +529,8 @@
         "ntd,dkc->ntkc", hidden, base_key_value_weight, preferred_element_type=jnp.float32
     ).reshape(requests, 2, 2 * width)
     received = {}
-    first_parts = layout
+    first_parts = layout[1:] if len(layout) > 1 else layout
+    near = layout[0]
     ready = gate(
         [packed[part] for part in first_parts],
         pieces[replicas // 2], pieces[1], both, both_ids, base,
@@ -524,58 +552,61 @@
         .transpose(0, 2, 1, 3, 4)
         .reshape(requests, heads, 2 * group_size, HEAD_WIDTH)
     )
+    (late_destination,) = gate([destination], mark)
     order = jnp.arange(requests)
-    same = destination[:, None] == destination[None, :]
+    same = late_destination[:, None] == late_destination[None, :]
     arrival = jnp.sum((same & (order[None, :] < order[:, None])).astype(jnp.int32), 1)
-    place = destination * pairs + arrival
+    place = late_destination * pairs + arrival
     slots = replicas * pairs
+    place, query, other_placement, cos, sin = gate([place, query, other_placement, cos, sin], mark)
 
     def serve():
-        first, second, first_send, second_send, products = adapt(
+        first, second, first_send, second_send, low, products = adapt(
             me, group_at, placement, other_placement, both_ids, both, pieces, half, extra, both
         )
-        low = products[: 2 * requests] + exchange(products[2 * requests :], "groups", 1)
+        low = low + exchange(products, "groups", 1)
         second_other = exchange(second_send, "groups", 1)
-        (first_send,) = gate([first_send], low, second_other)
+        first_send, close = gate([first_send, packed[near]], low, second_other)
+        close = exchange(close, "replica", 1)
         first_other = exchange(first_send, "groups", 1)
-        resident_first = place_half(group_at, first_other, first)
         theirs = second_other.reshape(hot, rank, width)
         bit = 1
-        while bit < tensor:
+        while 2 * bit < tensor:
             low = low + exchange(low, "tensor", bit)
             bit *= 2
-        low = low.astype(jnp.bfloat16).reshape(requests, 2, rank2)
         ours = second.reshape(hot, rank, width)
+        lows = (low, exchange(low, "tensor", bit))
+        small = attend(
+            place, counts, request_hot_entry, group_at, lows, ours, theirs, base, cos, sin, query,
+            earlier_token_cache, slots,
+        )
         resident = jnp.where(
             group == 0, jnp.stack([ours, theirs], 1), jnp.stack([theirs, ours], 1)
         )
+        smalls = lax.all_to_all(
+            small.reshape((replicas, pairs) + small.shape[1:]), "replica", 0, 0, tiled=True
+        )
         (out,) = unpack(
-            me, dest_all, count_all, earlier_token_cache, {}, None, None, pairs, context, None
-        )
-        small = attend(
-            place, counts, request_hot_entry, low, resident, base, cos, sin, query,
-            earlier_token_cache, slots, out,
-        )
-        small = small.reshape(replicas, pairs, TILE, width + LANES)
-        smalls = lax.all_to_all(small, "replica", 0, 0, tiled=True)
-        return smalls, resident_first, resident, out
+            me, dest_all, count_all, earlier_token_cache, {}, None, None, pairs, context, small
+        )
+        resident_first = place_half(group_at, first_other, first, out)
+        (out,) = unpack(
+            me, dest_all, count_all, None, {near: close}, None, out, pairs, context,
+            resident_first,
+        )
+        return resident_first, resident, out, smalls
 
     def nothing():
         return (
-            jnp.zeros((replicas, pairs, TILE, width + LANES), jnp.bfloat16),
             jnp.zeros((hot, piece, rank2), jnp.bfloat16),
             jnp.zeros((hot, 2, rank, width), jnp.bfloat16),
             jnp.zeros((slots, 2, context, width), jnp.bfloat16),
-        )
-
-    smalls, resident_first, resident_second, out = lax.cond(always, serve, nothing)
-    moved_cache, attended = unpack(
-        me, dest_all, count_all, None, received, smalls, out, pairs, context, resident_first
-    )
-    moved_attention = (
-        attended.reshape(slots, 2, group_size, heads, HEAD_WIDTH)
-        .transpose(0, 1, 3, 2, 4)
-        .reshape(slots, 2, group_size * width)
+            jnp.zeros((replicas, pairs, 2, (group_size + 2) * width), jnp.bfloat16),
+        )
+
+    resident_first, resident_second, out, smalls = lax.cond(always, serve, nothing)
+    moved_cache, moved_attention = unpack(
+        me, dest_all, count_all, None, received, smalls, out, pairs, context, both
     )
     return (moved_cache, moved_attention, resident_first, resident_second)
 

time: 120 us -> 114 us (0.950)
  waiting for transfers between devices: 40 us -> 35 us
    all_to_all x1, waiting for transfers between devices: 2.7 us -> 0.01 us  [serve(): lax.all_to_all(small.reshape((replicas, pairs) + small.shape[1:]), 'repli...]
    ppermute x12, waiting for transfers between devices: 37.3 us -> 35 us  [exchange(): return lax.ppermute(values, axis, [(i, i ^ mask) for i in range(size)])]
    reshape x2, local copies, waits for them, and re-layouts: 0.68 us -> 2.98 us  [per_device(): queries.reshape(requests, 2, heads, group_size, HEAD_WIDTH)]
    reshape x2 -> x0, local copies, waits for them, and re-layouts: 2.09 us -> none  [the longest x1 1.49 us: per_device(): moved_attention = attended.reshape(slots, 2, group_size, heads, HEAD_WIDT...]
    cond x18 -> x15, local copies, waits for them, and re-layouts: 1.65 us -> 2.97 us
    pallas_call x2 -> x3, Pallas kernels: 8 us -> 8.77 us  [unpack(): pl.pallas_call(functools.partial(unpack_kernel, layout, own, fill, tail,...]
  transfers between devices with their start and end apart: 13 -> 13, of which waited for: 6 -> 6; matrix products, arithmetic and copies ran while one was open for 20% -> 21% of each run, Pallas kernels for 19% -> 21%
where the time goes in v1:
time: 114 us; the launch traced here: 113 us
  waiting for transfers between devices  35 us (31%)
  Pallas kernels  27.1 us (24%)
  starting transfers between devices  21.2 us (19%)
  local copies, waits for them, and re-layouts  12.3 us (11%)
  other arithmetic  11.5 us (10%)
  matrix products  4.61 us (4%)
    ppermute x12, waiting for transfers between devices, exchange(): return lax.ppermute(values, axis, [(i, i ^ mask) for i in range(size)])  35 us
    ppermute x12, starting transfers between devices, exchange(): return lax.ppermute(values, axis, [(i, i ^ mask) for i in range(size)])  16.5 us
    pallas_call x1, Pallas kernels, attend(): pl.pallas_call(attend_kernel, out_shape=jax.ShapeDtypeStruct((slots, 2, (...  9.02 us
    pallas_call x3, Pallas kernels, unpack(): pl.pallas_call(functools.partial(unpack_kernel, layout, own, fill, tail,...  8.77 us
    all_to_all x1, starting transfers between devices, serve(): lax.all_to_all(small.reshape((replicas, pairs) + small.shape[1:]), 'repli...  4.66 us
    dot_general x1, matrix products, per_device(): jnp.einsum('ntd,dkc->ntkc', hidden, base_key_value_weight, preferred_elem...  4.61 us
    pallas_call x1, Pallas kernels, pack(): pl.pallas_call(functools.partial(pack_kernel, layout, live), out_shape=[j...  3.88 us
    pallas_call x1, Pallas kernels, adapt(): pl.pallas_call(functools.partial(adapt_kernel, half, extra, len(pieces)),...  3.2 us
  transfers between devices with their start and end apart: 13, of which 6 were waited for; matrix products, arithmetic and copies ran while one was open for 21% of the time, Pallas kernels for 21%

profile of v1, /device:TPU:0, one launch (start us, length us, event | category | flops | bytes accessed | tf_op | source)
XLA Modules:
  0.0 112.6 jit_solution(10879747119033848347)
XLA Ops:
  0.7 0.8 copy.88.dest_ref.refs_0_
  1.4 0.7 convert.19
  2.2 0.8 dynamic-slice_bitcast_fusion.1
  3.1 4.1 %collective-permute-start.7 = (bf16[1168,256]{1,0:T(8,128)(2,1)S(1)}, bf16[1168,256]{1,0:T(8,128)(2,1)S(1)}, u32[]{:S(2)}, u32[]{:S(2)}) collective-permute-start(bf16[1168,256]{1,0:T(8,128)(2,1)S(1)} %pad_maximum_fusion), channel_id=1, source_target_pairs={{0,8},{4,12},{8,0},{12,4},{1,9},{5,13},{9,1},{13,5},{2,10},{6,14},... | collective-permute-start | bytes 1794056 | tf_op jit(solution)/shard_map/ppermute | solution.py:23
  7.2 1.6 %collective-permute-start.6 = (bf16[1168,256]{1,0:T(8,128)(2,1)S(1)}, bf16[1168,256]{1,0:T(8,128)(2,1)S(1)}, u32[]{:S(2)}, u32[]{:S(2)}) collective-permute-start(bf16[1168,256]{1,0:T(8,128)(2,1)S(1)} %pad_maximum_fusion), channel_id=1, source_target_pairs={{0,4},{4,0},{8,12},{12,8},{1,5},{5,1},{9,13},{13,9},{2,6},{6,2},{1... | collective-permute-start | bytes 1794056 | tf_op jit(solution)/shard_map/ppermute | solution.py:23
  8.8 0.7 compare_select_fusion
  9.5 0.7 convert.22
  10.1 1.3 %gather_fusion = s32[8]{0:T(128)S(1)} fusion(s32[2]{0:T(128)} %param.18, s32[1024]{0:T(1024)S(1)} %pad_clamp_fusion), kind=kCustom, calls=%fused_computation | custom fusion | bytes 96 | tf_op jit(solution)/shard_map/gather | solution.py:513
  11.8 1.1 reshape.107
  12.9 0.6 fusion.5.refs_0_
  13.6 3.9 %pack.1 = (bf16[6,2,128,256]{3,2,1,0:T(8,128)(2,1)}, bf16[6,2,128,256]{3,2,1,0:T(8,128)(2,1)}, bf16[6,2,128,256]{3,2,1,0:T(8,128)(2,1)}, f32[8,128]{1,0:T(8,128)}) custom-call(s32[1]{0:T(128)} %bitcast.4.me_ref.refs_0_, s32[8]{0:T(128)} %copy-done.13, s32[8]{0:T(128)} %bitcast.34, bf16[8,2,512,256]{3,2,1,0:T(8,128)(2,1)} %cache_ref.1), custom_call_target="tpu_custom_call" | custom-call | flops 1 | bytes 1 | tf_op jit(solution)/shard_map/pack/pallas_call | solution.py:88
  17.5 1.6 %collective-permute-start.9 = (bf16[16,1152]{1,0:T(8,128)(2,1)}, bf16[16,1152]{1,0:T(8,128)(2,1)S(1)}, u32[]{:S(2)}, u32[]{:S(2)}) collective-permute-start(bf16[16,1152]{1,0:T(8,128)(2,1)} %gate.6), channel_id=1, source_target_pairs={{0,16},{16,0},{1,17},{17,1},{2,18},{18,2},{3,19},{19,3},{4,20},{20... | collective-permute-start | bytes 110600 | tf_op jit(solution)/shard_map/ppermute | solution.py:23
  19.1 4.6 %fusion = f32[8,2,2,256]{3,0,2,1:T(8,128)S(1)} fusion(bf16[8192,2,256]{2,1,0:T(2,128)(2,1)} %param.19, bf16[8,2,8192,1]{2,1,0,3:T(2,128)(2,1)S(1)} %bitcast.30), kind=kOutput, calls=%fused_computation.2 | convolution fusion | flops 134217728 | bytes 8683520 | tf_op jit(solution)/shard_map/ntd,dkc->ntkc/dot_general | solution.py:528
  23.8 0.8 fusion.14
  24.6 1.4 %convert_reduce_fusion.1 = s32[8]{0:T(128)} fusion(s32[8]{0:T(128)} %gate.8), kind=kLoop, calls=%fused_computation.29 | loop fusion | flops 312 | bytes 64 | tf_op jit(solution)/shard_map/reduce_sum | solution.py:558
  26.9 6.8 %collective-permute-done.7.refs_2_ = bf16[1168,256]{1,0:T(8,128)(2,1)S(1)} collective-permute-done((bf16[1168,256]{1,0:T(8,128)(2,1)S(1)}, bf16[1168,256]{1,0:T(8,128)(2,1)S(1)}, u32[]{:S(2)}, u32[]{:S(2)}) %collective-permute-start.7) | collective-permute-done | bytes 598048 | tf_op jit(solution)/shard_map/ppermute | solution.py:23
  33.6 0.6 collective-permute-start.8
  34.3 0.7 broadcast_in_dim.20.refs_5_
  35.0 3.4 %collective-permute-start.10 = (bf16[6,2,128,256]{3,2,1,0:T(8,128)(2,1)}, bf16[6,2,128,256]{3,2,1,0:T(8,128)(2,1)}, u32[]{:S(2)}, u32[]{:S(2)}) collective-permute-start(bf16[6,2,128,256]{3,2,1,0:T(8,128)(2,1)} %get-tuple-element.97), channel_id=1, source_target_pairs={{0,8},{4,12},{8,0},{12,4},{1,9},{5,13},{9,1},{13,5},{2,10},{6,14},... | collective-permute-start | bytes 2359304 | tf_op jit(solution)/shard_map/ppermute | solution.py:23
  38.8 1.5 %pad_maximum_fusion.2 = (f32[8,2,128]{2,1,0:T(2,128)S(1)}, f32[8,2,128]{2,1,0:T(2,128)}) fusion(f32[8,2,64]{2,1,0:T(2,128)} %get-tuple-element.132, f32[8,2,64]{2,1,0:T(2,128)} %get-tuple-element.131, f32[8,2,64]{2,1,0:T(2,128)} %get-tuple-element.130), kind=kLoop, calls=%fused_computation.24 | loop fusion | flops 4096 | bytes 28672 | tf_op jit(solution)/shard_map/concatenate | solution.py:547
  40.3 1.5 %reshape.110 = bf16[8,2,2,8,128]{4,3,2,1,0:T(8,128)(2,1)} reshape(bf16[8,2,2048]{2,1,0:T(2,128)(2,1)} %param.13) | data formatting | bytes 131072 | tf_op jit(solution)/shard_map/reshape | solution.py:551
  41.8 1.5 %copy.64 = bf16[8,2,2,8,128]{4,3,1,2,0:T(8,128)(2,1)} copy(bf16[8,2,2,8,128]{4,3,2,1,0:T(8,128)(2,1)} %reshape.110) | data formatting | bytes 131072 | tf_op jit(solution)/shard_map/reshape | solution.py:551
  43.3 0.7 multiply_add_fusion.refs_0_
  43.9 1.3 %fusion.13.refs_2_ = s32[2]{0:T(128)} fusion(bf16[16,1152]{1,0:T(8,128)(2,1)} %copy-done.8), kind=kLoop, calls=%fused_computation.38 | loop fusion | flops 2 | bytes 12 | tf_op jit(solution)/shard_map/convert_element_type | solution.py:522
  45.2 14.7 %collective-permute-done.8 = bf16[1168,256]{1,0:T(8,128)(2,1)S(1)} collective-permute-done((bf16[1168,256]{1,0:T(8,128)(2,1)S(1)}, bf16[1168,256]{1,0:T(8,128)(2,1)S(1)}, u32[]{:S(2)}, u32[]{:S(2)}) %collective-permute-start.8) | collective-permute-done | bytes 598048 | tf_op jit(solution)/shard_map/ppermute | solution.py:23
  59.9 0.7 maximum_convert_fusion
  60.6 0.6 fusion.15
  61.2 48.2 %conditional.1 = (bf16[2,2048,256]{2,1,0:T(8,128)(2,1)}, bf16[8,2,512,256]{3,2,1,0:T(8,128)(2,1)}, bf16[4,2,2,2560]{3,2,1,0:T(2,128)(2,1)}, bf16[2,2,128,256]{3,2,1,0:T(8,128)(2,1)}) conditional(s32[]{:T(128)} %bitcast.11, () %tuple.16, (s32[]{:T(128)}, s32[1]{0:T(128)}, s32[2]{0:T(128)S(1)}, s32[2]{0:T(128)}, s32[32,256]{1,0:T(8,128)}, ...), branch_computations={%region_1.2_spmd, %region_2.3_spmd} | conditional | flops 401415 | bytes 15352836 | solution.py:607
  61.2 3.2 %adapt.1 = (bf16[2,2048,256]{2,1,0:T(8,128)(2,1)}, bf16[2,128,256]{2,1,0:T(8,128)(2,1)}, bf16[2,1024,256]{2,1,0:T(8,128)(2,1)}, bf16[2,128,256]{2,1,0:T(8,128)(2...) custom-call(s32[1]{0:T(128)} %get-tuple-element.45.me_ref.refs_0_, s32[2]{0:T(128)S(1)} %get-tuple-element.46.own_ref, ...), custom_call_target="tpu_custom_call" | custom-call | flops 1 | bytes 1 | tf_op jit(solution)/shard_map/cond/branch_1_fun/adapt/pallas_call | solution.py:313
  64.5 1.3 %collective-permute-start.1 = (bf16[2,128,256]{2,1,0:T(8,128)(2,1)}, bf16[2,128,256]{2,1,0:T(8,128)(2,1)S(1)}, u32[]{:S(2)}, u32[]{:S(2)}) collective-permute-start(bf16[2,128,256]{2,1,0:T(8,128)(2,1)} %get-tuple-element.58), channel_id=1, source_target_pairs={{0,16},{16,0},{1,17},{17,1},{2,18},{18,2},{3,19},{19,3},{4,20},{20... | collective-permute-start | bytes 393224 | tf_op jit(solution)/shard_map/cond/branch_1_fun/ppermute | solution.py:23
  65.8 0.7 collective-permute-start
  66.6 3.3 %collective-permute-done = f32[16,256]{1,0:T(8,128)S(1)} collective-permute-done((f32[16,256]{1,0:T(8,128)}, f32[16,256]{1,0:T(8,128)S(1)}, u32[]{:S(2)}, u32[]{:S(2)}) %collective-permute-start) | collective-permute-done | bytes 16416 | tf_op jit(solution)/shard_map/cond/branch_1_fun/ppermute | solution.py:23
  69.9 1.3 %add.35.refs_2_ = f32[16,256]{1,0:T(8,128)} add(f32[16,256]{1,0:T(8,128)} %get-tuple-element.56, f32[16,256]{1,0:T(8,128)S(1)} %collective-permute-done) | non-fusion elementwise | flops 4096 | bytes 49152 | tf_op jit(solution)/shard_map/cond/branch_1_fun/add | solution.py:567
  71.2 0.7 copy-done.2
  71.9 1.3 %collective-permute-start.2 = (bf16[2,1024,256]{2,1,0:T(8,128)(2,1)}, bf16[2,1024,256]{2,1,0:T(8,128)(2,1)S(1)}, u32[]{:S(2)}, u32[]{:S(2)}) collective-permute-start(bf16[2,1024,256]{2,1,0:T(8,128)(2,1)} %get-tuple-element.59), channel_id=1, source_target_pairs={{0,16},{16,0},{1,17},{17,1},{2,18},{18,2},{3,19},{19,3},{4,20},{20... | collective-permute-start | bytes 3145736 | tf_op jit(solution)/shard_map/cond/branch_1_fun/ppermute | solution.py:23
  73.2 1.4 %collective-permute-done.3 = f32[16,256]{1,0:T(8,128)S(1)} collective-permute-done((f32[16,256]{1,0:T(8,128)}, f32[16,256]{1,0:T(8,128)S(1)}, u32[]{:S(2)}, u32[]{:S(2)}) %collective-permute-start.3) | collective-permute-done | bytes 16416 | tf_op jit(solution)/shard_map/cond/branch_1_fun/ppermute | solution.py:23
  74.5 0.7 add.36.low_ref
  75.3 1.5 %collective-permute-start.4 = (f32[16,256]{1,0:T(8,128)S(1)}, f32[16,256]{1,0:T(8,128)S(1)}, u32[]{:S(2)}, u32[]{:S(2)}) collective-permute-start(f32[16,256]{1,0:T(8,128)S(1)} %add.36.low_ref), channel_id=1, source_target_pairs={{0,2},{1,3},{2,0},{3,1},{4,6},{5,7},{6,4},{7,5},{8,10},{9,11},{10,... | collective-permute-start | bytes 49160 | tf_op jit(solution)/shard_map/cond/branch_1_fun/ppermute | solution.py:23
  76.8 2.2 %collective-permute-done.4.low_other_ref = f32[16,256]{1,0:T(8,128)S(1)} collective-permute-done((f32[16,256]{1,0:T(8,128)S(1)}, f32[16,256]{1,0:T(8,128)S(1)}, u32[]{:S(2)}, u32[]{:S(2)}) %collective-permute-start.4) | collective-permute-done | bytes 16416 | tf_op jit(solution)/shard_map/cond/branch_1_fun/ppermute | solution.py:23
  79.6 9.0 %attend.1.refs_4_ = bf16[8,2,2560]{2,1,0:T(2,128)(2,1)} custom-call(s32[8]{0:T(128)} %get-tuple-element.64.place_ref, s32[8]{0:T(128)} %get-tuple-element.65.count_ref, s32[8]{0:T(128)} %get-tuple-element.66.hot_ref, s32[1]{0:T(128)} %bitcast.group_ref, f32[16,256]{1,0:T(8,128)} %copy-done.7, f32[16,256]{1,0:T(8,128)} %copy-done.10, ...), custom_call_target="tpu_custom_call" | custom-call | flops 1 | bytes 1 | tf_op jit(solution)/shard_map/cond/branch_1_fun/attend/pallas_call | solution.py:431
  88.6 4.7 %all-to-all-start = ((bf16[4,2,2,2560]{3,2,1,0:T(2,128)(2,1)}), bf16[4,2,2,2560]{3,2,1,0:T(2,128)(2,1)}, u32[]{:S(2)}, u32[]{:S(2)}) async-start(bf16[4,2,2,2560]{3,2,1,0:T(2,128)(2,1)} %bitcast.31), calls=%async_computation | async-start | bytes 163840 | tf_op jit(solution)/shard_map/cond/branch_1_fun/all_to_all | solution.py:586
  93.3 3.6 %unpack.3.after_ref.refs_4_ = bf16[8,2,512,256]{3,2,1,0:T(8,128)(2,1)} custom-call(s32[1]{0:T(128)} %get-tuple-element.45.me_ref.refs_0_, s32[4,8]{1,0:T(4,128)S(1)} %copy-done.9, s32[4,8]{1,0:T(4,128)S(1)} %get-tuple-element.62.refs_2_, bf16[8,2,512,256]{3,2,1,0:T(8,128)(2,1)} %get-tuple-element.63.cache_ref.refs_3_, bf16[8,2,2560]{2,1,0:T(2,128)(2,1)} %attend.1.refs_4_), custom_call_target="tpu_custom_call" | custom-call | flops 1 | bytes 1 | tf_op jit(solution)/shard_map/cond/branch_1_fun/unpack/pallas_call | solution.py:261
  97.0 0.7 copy.56
  97.7 1.0 copy-done.4
  98.7 2.2 %place_half.1.refs_5_ = bf16[2,2048,256]{2,1,0:T(8,128)(2,1)} custom-call(s32[1]{0:T(128)} %bitcast.group_ref, bf16[2,1024,256]{2,1,0:T(8,128)(2,1)} %copy-done.4, bf16[2,2048,256]{2,1,0:T(8,128)(2,1)} %get-tuple-element.60._, bf16[8,2,512,256]{3,2,1,0:T(8,128)(2,1)} %unpack.3.after_ref.refs_4_), custom_call_target="tpu_custom_call", output_to_operand_aliasing={{}: (2, {})} | custom-call | flops 1 | bytes 1 | tf_op jit(solution)/shard_map/cond/branch_1_fun/place_half/pallas_call | solution.py:340
  100.9 6.5 %collective-permute-done.5.refs_3_ = bf16[6,2,128,256]{3,2,1,0:T(8,128)(2,1)} collective-permute-done((bf16[6,2,128,256]{3,2,1,0:T(8,128)(2,1)}, bf16[6,2,128,256]{3,2,1,0:T(8,128)(2,1)}, u32[]{:S(2)}, u32[]{:S(2)}) %collective-permute-start.5) | collective-permute-done | bytes 786464 | tf_op jit(solution)/shard_map/cond/branch_1_fun/ppermute | solution.py:23
  107.4 2.0 %unpack.4 = bf16[8,2,512,256]{3,2,1,0:T(8,128)(2,1)} custom-call(s32[1]{0:T(128)} %get-tuple-element.45.me_ref.refs_0_, s32[4,8]{1,0:T(4,128)S(1)} %copy-done.9, s32[4,8]{1,0:T(4,128)S(1)} %get-tuple-element.62.refs_2_, bf16[6,2,128,256]{3,2,1,0:T(8,128)(2,1)} %collective-permute-done.5.refs_3_, ...), custom_call_target="tpu_custom_call", output_to_operand_aliasing={{}: (4, {})} | custom-call | flops 1 | bytes 1 | tf_op jit(solution)/shard_map/cond/branch_1_fun/unpack/pallas_call | solution.py:261
  109.4 3.2 %unpack.5 = (bf16[8,2,512,256]{3,2,1,0:T(8,128)(2,1)}, bf16[8,2,2048]{2,1,0:T(2,128)(2,1)}) custom-call(s32[1]{0:T(128)} %bitcast.4.me_ref.refs_0_, s32[4,8]{1,0:T(4,128)} %get-tuple-element.134.refs_1_, s32[4,8]{1,0:T(4,128)S(1)} %get-tuple-element.133.refs_2_, ...), custom_call_target="tpu_custom_call", output_to_operand_aliasing={{0}: (6, {})} | custom-call | flops 1 | bytes 1 | tf_op jit(solution)/shard_map/unpack/pallas_call | solution.py:261
  (72 shorter events, 2.7 us)
Async XLA Ops:
  0.6 2.4 %copy-start = (bf16[1,2048,256]{2,1,0:T(8,128)(2,1)S(1)}, bf16[1,2048,256]{2,1,0:T(8,128)(2,1)}, u32[]{:S(2)}) copy-start(bf16[1,2048,256]{2,1,0:T(8,128)(2,1)} %param.20) | copy-start | bytes 3145732
  0.6 18.5 %copy-start.5 = (bf16[8,2,8192]{2,1,0:T(2,128)(2,1)S(1)}, bf16[8,2,8192]{2,1,0:T(2,128)(2,1)}, u32[]{:S(2)}) copy-start(bf16[8,2,8192]{2,1,0:T(2,128)(2,1)} %param.12) | copy-start | bytes 786436
  0.7 18.4 %copy-start.11 = (s32[1,8]{1,0:T(1,128)S(1)}, s32[1,8]{1,0:T(1,128)}, u32[]{:S(2)}) copy-start(s32[1,8]{1,0:T(1,128)} %param.15) | copy-start | bytes 100
  1.4 12.1 %copy-start.13 = (s32[8]{0:T(128)}, s32[8]{0:T(128)S(1)}, u32[]{:S(2)}) copy-start(s32[8]{0:T(128)S(1)} %copy.88.dest_ref.refs_0_) | copy-start | bytes 100
  1.4 8.0 %copy-start.14 = (bf16[1,8]{1,0:T(2,128)(2,1)}, bf16[1,8]{1,0:T(2,128)(2,1)S(1)}, u32[]{:S(2)}) copy-start(bf16[1,8]{1,0:T(2,128)(2,1)S(1)} %convert_bitcast_fusion) | copy-start | bytes 52
  2.1 21.6 %copy-start.15 = (bf16[1,8]{1,0:T(2,128)(2,1)}, bf16[1,8]{1,0:T(2,128)(2,1)S(1)}, u32[]{:S(2)}) copy-start(bf16[1,8]{1,0:T(2,128)(2,1)S(1)} %convert.19) | copy-start | bytes 52
  3.1 30.5 %collective-permute-start.7 = (bf16[1168,256]{1,0:T(8,128)(2,1)S(1)}, bf16[1168,256]{1,0:T(8,128)(2,1)S(1)}, u32[]{:S(2)}, u32[]{:S(2)}) collective-permute-start(bf16[1168,256]{1,0:T(8,128)(2,1)S(1)} %pad_maximum_fusion), channel_id=1, source_target_pairs={{0,8},{4,12},{8,0},{12,4},{1,9},{5,13},{9,1},{13,5},{2,10},{6,14},... | collective-permute-start | bytes 1794056 | tf_op jit(solution)/shard_map/ppermute | solution.py:23
  7.2 27.1 %collective-permute-start.6 = (bf16[1168,256]{1,0:T(8,128)(2,1)S(1)}, bf16[1168,256]{1,0:T(8,128)(2,1)S(1)}, u32[]{:S(2)}, u32[]{:S(2)}) collective-permute-start(bf16[1168,256]{1,0:T(8,128)(2,1)S(1)} %pad_maximum_fusion), channel_id=1, source_target_pairs={{0,4},{4,0},{8,12},{12,8},{1,5},{5,1},{9,13},{13,9},{2,6},{6,2},{1... | collective-permute-start | bytes 1794056 | tf_op jit(solution)/shard_map/ppermute | solution.py:23
  17.5 8.8 %collective-permute-start.9 = (bf16[16,1152]{1,0:T(8,128)(2,1)}, bf16[16,1152]{1,0:T(8,128)(2,1)S(1)}, u32[]{:S(2)}, u32[]{:S(2)}) collective-permute-start(bf16[16,1152]{1,0:T(8,128)(2,1)} %gate.6), channel_id=1, source_target_pairs={{0,16},{16,0},{1,17},{17,1},{2,18},{18,2},{3,19},{19,3},{4,20},{20... | collective-permute-start | bytes 110600 | tf_op jit(solution)/shard_map/ppermute | solution.py:23
  19.1 42.1 %copy-start.1 = (s32[2]{0:T(128)S(1)}, s32[2]{0:T(128)}, u32[]{:S(2)}) copy-start(s32[2]{0:T(128)} %param.18) | copy-start | bytes 28
  26.2 0.6 copy-start.8
  33.6 26.2 %collective-permute-start.8 = (bf16[1168,256]{1,0:T(8,128)(2,1)S(1)}, bf16[1168,256]{1,0:T(8,128)(2,1)S(1)}, u32[]{:S(2)}, u32[]{:S(2)}) collective-permute-start(bf16[1168,256]{1,0:T(8,128)(2,1)S(1)} %collective-permute-done.7.refs_2_), channel_id=1, source_target_pairs={{0,4},{4,0},{8,12},{12,8},{1,5},{5,1},{9,13},{13,9},{2,6},{6,2},{1... | collective-permute-start | bytes 1794056 | tf_op jit(solution)/shard_map/ppermute | solution.py:23
  35.0 74.4 %collective-permute-start.10 = (bf16[6,2,128,256]{3,2,1,0:T(8,128)(2,1)}, bf16[6,2,128,256]{3,2,1,0:T(8,128)(2,1)}, u32[]{:S(2)}, u32[]{:S(2)}) collective-permute-start(bf16[6,2,128,256]{3,2,1,0:T(8,128)(2,1)} %get-tuple-element.97), channel_id=1, source_target_pairs={{0,8},{4,12},{8,0},{12,4},{1,9},{5,13},{9,1},{13,5},{2,10},{6,14},... | collective-permute-start | bytes 2359304 | tf_op jit(solution)/shard_map/ppermute | solution.py:23
  38.4 71.0 %collective-permute-start.11 = (bf16[6,2,128,256]{3,2,1,0:T(8,128)(2,1)}, bf16[6,2,128,256]{3,2,1,0:T(8,128)(2,1)}, u32[]{:S(2)}, u32[]{:S(2)}) collective-permute-start(bf16[6,2,128,256]{3,2,1,0:T(8,128)(2,1)} %get-tuple-element.98), channel_id=1, source_target_pairs={{0,12},{4,8},{8,4},{12,0},{1,13},{5,9},{9,5},{13,1},{2,14},{6,10},... | collective-permute-start | bytes 2359304 | tf_op jit(solution)/shard_map/ppermute | solution.py:23
  45.2 14.7 %copy-start.12 = (s32[8]{0:T(128)}, s32[8]{0:T(128)S(1)}, u32[]{:S(2)}) copy-start(s32[8]{0:T(128)S(1)} %get-tuple-element.101) | copy-start | bytes 100
  64.4 28.9 %copy-start.9 = (s32[4,8]{1,0:T(4,128)S(1)}, s32[4,8]{1,0:T(4,128)}, u32[]{:S(2)}) copy-start(s32[4,8]{1,0:T(4,128)} %get-tuple-element.61.refs_1_) | copy-start | bytes 388 | tf_op jit(solution)/shard_map/cond
  64.5 6.7 %collective-permute-start.1 = (bf16[2,128,256]{2,1,0:T(8,128)(2,1)}, bf16[2,128,256]{2,1,0:T(8,128)(2,1)S(1)}, u32[]{:S(2)}, u32[]{:S(2)}) collective-permute-start(bf16[2,128,256]{2,1,0:T(8,128)(2,1)} %get-tuple-element.58), channel_id=1, source_target_pairs={{0,16},{16,0},{1,17},{17,1},{2,18},{18,2},{3,19},{19,3},{4,20},{20... | collective-permute-start | bytes 393224 | tf_op jit(solution)/shard_map/cond/branch_1_fun/ppermute | solution.py:23
  65.8 4.1 %collective-permute-start = (f32[16,256]{1,0:T(8,128)}, f32[16,256]{1,0:T(8,128)S(1)}, u32[]{:S(2)}, u32[]{:S(2)}) collective-permute-start(f32[16,256]{1,0:T(8,128)} %get-tuple-element.57), channel_id=1, source_target_pairs={{0,16},{16,0},{1,17},{17,1},{2,18},{18,2},{3,19},{19,3},{4,20},{20... | collective-permute-start | bytes 49160 | tf_op jit(solution)/shard_map/cond/branch_1_fun/ppermute | solution.py:23
  71.2 0.7 copy-start.2
  71.9 25.8 %collective-permute-start.2 = (bf16[2,1024,256]{2,1,0:T(8,128)(2,1)}, bf16[2,1024,256]{2,1,0:T(8,128)(2,1)S(1)}, u32[]{:S(2)}, u32[]{:S(2)}) collective-permute-start(bf16[2,1024,256]{2,1,0:T(8,128)(2,1)} %get-tuple-element.59), channel_id=1, source_target_pairs={{0,16},{16,0},{1,17},{17,1},{2,18},{18,2},{3,19},{19,3},{4,20},{20... | collective-permute-start | bytes 3145736 | tf_op jit(solution)/shard_map/cond/branch_1_fun/ppermute | solution.py:23
  73.1 34.3 %collective-permute-start.5 = (bf16[6,2,128,256]{3,2,1,0:T(8,128)(2,1)}, bf16[6,2,128,256]{3,2,1,0:T(8,128)(2,1)}, u32[]{:S(2)}, u32[]{:S(2)}) collective-permute-start(bf16[6,2,128,256]{3,2,1,0:T(8,128)(2,1)} %get-tuple-element.72), channel_id=1, source_target_pairs={{0,4},{4,0},{8,12},{12,8},{1,5},{5,1},{9,13},{13,9},{2,6},{6,2},{1... | collective-permute-start | bytes 2359304 | tf_op jit(solution)/shard_map/cond/branch_1_fun/ppermute | solution.py:23
  73.2 1.4 %collective-permute-start.3 = (f32[16,256]{1,0:T(8,128)}, f32[16,256]{1,0:T(8,128)S(1)}, u32[]{:S(2)}, u32[]{:S(2)}) collective-permute-start(f32[16,256]{1,0:T(8,128)} %add.35.refs_2_), channel_id=1, source_target_pairs={{0,1},{1,0},{2,3},{3,2},{4,5},{5,4},{6,7},{7,6},{8,9},{9,8},{10,11... | collective-permute-start | bytes 49160 | tf_op jit(solution)/shard_map/cond/branch_1_fun/ppermute | solution.py:23
  75.3 3.7 %copy-start.7 = (f32[16,256]{1,0:T(8,128)}, f32[16,256]{1,0:T(8,128)S(1)}, u32[]{:S(2)}) copy-start(f32[16,256]{1,0:T(8,128)S(1)} %add.36.low_ref) | copy-start | bytes 49156 | tf_op jit(solution)/shard_map/cond
  75.3 3.7 %collective-permute-start.4 = (f32[16,256]{1,0:T(8,128)S(1)}, f32[16,256]{1,0:T(8,128)S(1)}, u32[]{:S(2)}, u32[]{:S(2)}) collective-permute-start(f32[16,256]{1,0:T(8,128)S(1)} %add.36.low_ref), channel_id=1, source_target_pairs={{0,2},{1,3},{2,0},{3,1},{4,6},{5,7},{6,4},{7,5},{8,10},{9,11},{10,... | collective-permute-start | bytes 49160 | tf_op jit(solution)/shard_map/cond/branch_1_fun/ppermute | solution.py:23
  79.0 0.6 copy-start.10
  88.6 20.8 %all-to-all-start = ((bf16[4,2,2,2560]{3,2,1,0:T(2,128)(2,1)}), bf16[4,2,2,2560]{3,2,1,0:T(2,128)(2,1)}, u32[]{:S(2)}, u32[]{:S(2)}) async-start(bf16[4,2,2,2560]{3,2,1,0:T(2,128)(2,1)} %bitcast.31), calls=%async_computation | async-start | bytes 163840 | tf_op jit(solution)/shard_map/cond/branch_1_fun/all_to_all | solution.py:586
  93.3 3.6 %copy-start.3 = (bf16[2,128,256]{2,1,0:T(8,128)(2,1)S(1)}, bf16[2,128,256]{2,1,0:T(8,128)(2,1)}, u32[]{:S(2)}) copy-start(bf16[2,128,256]{2,1,0:T(8,128)(2,1)} %copy-done.2) | copy-start | bytes 393220 | tf_op jit(solution)/shard_map/cond
  93.3 3.6 %copy-start.6 = (bf16[2,128,256]{2,1,0:T(8,128)(2,1)S(1)}, bf16[2,128,256]{2,1,0:T(8,128)(2,1)}, u32[]{:S(2)}) copy-start(bf16[2,128,256]{2,1,0:T(8,128)(2,1)} %get-tuple-element.67.ours_ref) | copy-start | bytes 393220 | tf_op jit(solution)/shard_map/cond
  97.7 1.0 copy-start.4

commit v2 on v1

--- a/solution.py
+++ b/solution.py
@@ -495,13 +495,9 @@
     info = jnp.pad(info[None], ((0, TILE - 1), (0, rank2 - info.shape[0])))
     pieces = {0: jnp.concatenate([first_half, second_half, info], 0)}
     bit = replicas // 2
-    while bit:
-        for mask in list(pieces):
-            pieces[mask ^ bit] = exchange(pieces[mask], "replica", bit)
-        bit //= 2
-    pieces = [pieces[mask] for mask in range(replicas)]
-    infos = jnp.stack([p[half + extra, : 2 * requests] for p in pieces]).astype(jnp.int32)
-    count_all, dest_all = infos[:, :requests], infos[:, requests:]
+    pieces[bit] = exchange(pieces[0], "replica", bit)
+    if bit > 1:
+        pieces[1] = exchange(pieces[0], "replica", 1)
 
     cap = live * pairs
     patterns = tuple(range(1, replicas))
@@ -528,17 +524,6 @@
     base = jnp.einsum(
         "ntd,dkc->ntkc", hidden, base_key_value_weight, preferred_element_type=jnp.float32
     ).reshape(requests, 2, 2 * width)
-    received = {}
-    first_parts = layout[1:] if len(layout) > 1 else layout
-    near = layout[0]
-    ready = gate(
-        [packed[part] for part in first_parts],
-        pieces[replicas // 2], pieces[1], both, both_ids, base,
-    )
-    for part, values in zip(first_parts, ready):
-        received[part] = exchange(values, "replica", part[0])
-    always = counts[0] > 0
-
     positions = (BLOCK * counts)[:, None] + jnp.arange(2)[None, :]
     half_size = HEAD_WIDTH // 2
     frequency = 10000.0 ** (-(jnp.arange(half_size, dtype=jnp.float32) * 2.0 / HEAD_WIDTH))
@@ -560,14 +545,40 @@
     slots = replicas * pairs
     place, query, other_placement, cos, sin = gate([place, query, other_placement, cos, sin], mark)
 
+    first_bit = replicas // 2
+    (pieces[first_bit],) = gate(
+        [pieces[first_bit]], both, both_ids, base, place, query, other_placement, cos, sin
+    )
+    bit = first_bit // 2
+    while bit:
+        for mask in sorted(pieces):
+            if mask ^ bit not in pieces:
+                pieces[mask ^ bit] = exchange(pieces[mask], "replica", bit)
+        bit //= 2
+    pieces = [pieces[mask] for mask in range(replicas)]
+    infos = jnp.stack([p[half + extra, : 2 * requests] for p in pieces]).astype(jnp.int32)
+    count_all, dest_all = infos[:, :requests], infos[:, requests:]
+    received = {}
+    first_parts = layout[1:] if len(layout) > 1 else layout
+    near = layout[0]
+    ready = gate(
+        [packed[part] for part in first_parts],
+        pieces[first_bit], pieces[1],
+    )
+    for part, values in zip(first_parts, ready):
+        received[part] = exchange(values, "replica", part[0])
+    (ready,) = gate([packed[near]], pieces[replicas - 1])
+    received[near] = exchange(ready, "replica", 1)
+    always = counts[0] > 0
+
+
     def serve():
         first, second, first_send, second_send, low, products = adapt(
             me, group_at, placement, other_placement, both_ids, both, pieces, half, extra, both
         )
         low = low + exchange(products, "groups", 1)
         second_other = exchange(second_send, "groups", 1)
-        first_send, close = gate([first_send, packed[near]], low, second_other)
-        close = exchange(close, "replica", 1)
+        (first_send,) = gate([first_send], low, second_other)
         first_other = exchange(first_send, "groups", 1)
         theirs = second_other.reshape(hot, rank, width)
         bit = 1
@@ -590,10 +601,6 @@
             me, dest_all, count_all, earlier_token_cache, {}, None, None, pairs, context, small
         )
         resident_first = place_half(group_at, first_other, first, out)
-        (out,) = unpack(
-            me, dest_all, count_all, None, {near: close}, None, out, pairs, context,
-            resident_first,
-        )
         return resident_first, resident, out, smalls
 
     def nothing():

time: 114 us -> 113 us (level)
  waiting for transfers between devices: 35 us -> 43.6 us
  other arithmetic: 11.5 us -> 7.85 us
  local copies, waits for them, and re-layouts: 12.3 us -> 8.97 us
  Pallas kernels: 27.1 us -> 25.3 us
    all_to_all x1, waiting for transfers between devices: 0.01 us -> 6.63 us  [serve(): lax.all_to_all(small.reshape((replicas, pairs) + small.shape[1:]), 'repli...]
    reshape x2, local copies, waits for them, and re-layouts: 2.98 us -> 0.06 us  [per_device(): queries.reshape(requests, 2, heads, group_size, HEAD_WIDTH)]
    ppermute x12, waiting for transfers between devices: 35 us -> 36.9 us  [exchange(): return lax.ppermute(values, axis, [(i, i ^ mask) for i in range(size)])]
    pallas_call x3 -> x2, Pallas kernels: 8.77 us -> 6.8 us  [unpack(): pl.pallas_call(functools.partial(unpack_kernel, layout, own, fill, tail,...]
    concatenate x1, other arithmetic: 1.45 us -> 0.09 us  [per_device(): cos = jnp.concatenate([cos, cos], -1)]
    convert_element_type x1, other arithmetic: 1.28 us -> 0.07 us  [per_device(): other_placement = theirs[0, half + 1:half + 1 + hot].astype(jnp.int32)]
  transfers between devices with their start and end apart: 13 -> 13, of which waited for: 6 -> 6; matrix products, arithmetic and copies ran while one was open for 21% -> 14% of each run, Pallas kernels for 21% -> 19%
where the time goes in v2:
time: 113 us; the launch traced here: 112 us
  waiting for transfers between devices  43.6 us (39%)
  Pallas kernels  25.3 us (22%)
  starting transfers between devices  20.9 us (18%)
  local copies, waits for them, and re-layouts  8.97 us (8%)
  other arithmetic  7.85 us (7%)
  matrix products  4.65 us (4%)
    ppermute x12, waiting for transfers between devices, exchange(): return lax.ppermute(values, axis, [(i, i ^ mask) for i in range(size)])  36.9 us
    ppermute x12, starting transfers between devices, exchange(): return lax.ppermute(values, axis, [(i, i ^ mask) for i in range(size)])  16.3 us
    pallas_call x1, Pallas kernels, attend(): pl.pallas_call(attend_kernel, out_shape=jax.ShapeDtypeStruct((slots, 2, (...  9.01 us
    pallas_call x2, Pallas kernels, unpack(): pl.pallas_call(functools.partial(unpack_kernel, layout, own, fill, tail,...  6.8 us
    all_to_all x1, waiting for transfers between devices, serve(): lax.all_to_all(small.reshape((replicas, pairs) + small.shape[1:]), 'repli...  6.63 us
    dot_general x1, matrix products, per_device(): jnp.einsum('ntd,dkc->ntkc', hidden, base_key_value_weight, preferred_elem...  4.65 us
    all_to_all x1, starting transfers between devices, serve(): lax.all_to_all(small.reshape((replicas, pairs) + small.shape[1:]), 'repli...  4.61 us
    pallas_call x1, Pallas kernels, pack(): pl.pallas_call(functools.partial(pack_kernel, layout, live), out_shape=[j...  4.02 us
  transfers between devices with their start and end apart: 13, of which 6 were waited for; matrix products, arithmetic and copies ran while one was open for 14% of the time, Pallas kernels for 19%

profile of v2, /device:TPU:0, one launch (start us, length us, event | category | flops | bytes accessed | tf_op | source)
XLA Modules:
  0.0 112.2 jit_solution(8328353585390375281)
XLA Ops:
  0.7 0.8 copy.88.dest_ref.refs_0_
  1.4 0.7 convert.19
  2.2 0.8 dynamic-slice_bitcast_fusion.1
  3.1 4.1 %collective-permute-start.6 = (bf16[1168,256]{1,0:T(8,128)(2,1)S(1)}, bf16[1168,256]{1,0:T(8,128)(2,1)S(1)}, u32[]{:S(2)}, u32[]{:S(2)}) collective-permute-start(bf16[1168,256]{1,0:T(8,128)(2,1)S(1)} %pad_maximum_fusion), channel_id=1, source_target_pairs={{0,8},{4,12},{8,0},{12,4},{1,9},{5,13},{9,1},{13,5},{2,10},{6,14},... | collective-permute-start | bytes 1794056 | tf_op jit(solution)/shard_map/ppermute | solution.py:23
  7.2 1.6 %collective-permute-start.5 = (bf16[1168,256]{1,0:T(8,128)(2,1)S(1)}, bf16[1168,256]{1,0:T(8,128)(2,1)S(1)}, u32[]{:S(2)}, u32[]{:S(2)}) collective-permute-start(bf16[1168,256]{1,0:T(8,128)(2,1)S(1)} %pad_maximum_fusion), channel_id=1, source_target_pairs={{0,4},{4,0},{8,12},{12,8},{1,5},{5,1},{9,13},{13,9},{2,6},{6,2},{1... | collective-permute-start | bytes 1794056 | tf_op jit(solution)/shard_map/ppermute | solution.py:23
  8.8 0.7 compare_select_fusion
  9.5 0.7 convert.22
  10.1 1.3 %gather_fusion = s32[8]{0:T(128)S(1)} fusion(s32[2]{0:T(128)} %param.18, s32[1024]{0:T(1024)S(1)} %pad_clamp_fusion), kind=kCustom, calls=%fused_computation | custom fusion | bytes 96 | tf_op jit(solution)/shard_map/gather | solution.py:509
  11.5 0.1 broadcast_in_dim_reshape.4
  11.7 0.1 copy.46
  11.8 1.1 reshape.106
  12.9 0.6 fusion.5.refs_0_
  13.6 4.0 %pack.1 = (bf16[6,2,128,256]{3,2,1,0:T(8,128)(2,1)}, bf16[6,2,128,256]{3,2,1,0:T(8,128)(2,1)}, bf16[6,2,128,256]{3,2,1,0:T(8,128)(2,1)}, f32[8,128]{1,0:T(8,128)}) custom-call(s32[1]{0:T(128)} %bitcast.4.me_ref.refs_0_, s32[8]{0:T(128)} %copy-done.17, s32[8]{0:T(128)} %bitcast.34, bf16[8,2,512,256]{3,2,1,0:T(8,128)(2,1)} %cache_ref.1), custom_call_target="tpu_custom_call" | custom-call | flops 1 | bytes 1 | tf_op jit(solution)/shard_map/pack/pallas_call | solution.py:88
  17.6 1.4 %collective-permute-start.7 = (bf16[16,1152]{1,0:T(8,128)(2,1)}, bf16[16,1152]{1,0:T(8,128)(2,1)S(1)}, u32[]{:S(2)}, u32[]{:S(2)}) collective-permute-start(bf16[16,1152]{1,0:T(8,128)(2,1)} %gate.8), channel_id=1, source_target_pairs={{0,16},{16,0},{1,17},{17,1},{2,18},{18,2},{3,19},{19,3},{4,20},{20... | collective-permute-start | bytes 110600 | tf_op jit(solution)/shard_map/ppermute | solution.py:23
  19.1 0.9 convert_reduce_fusion.1
  20.0 0.7 multiply_add_fusion.refs_0_
  20.7 0.2 fusion.14
  20.9 4.7 %fusion = f32[8,2,2,256]{3,0,2,1:T(8,128)S(1)} fusion(bf16[8192,2,256]{2,1,0:T(2,128)(2,1)} %param.19, bf16[8,2,8192,1]{2,1,0,3:T(2,128)(2,1)S(1)} %bitcast.31), kind=kOutput, calls=%fused_computation.2 | convolution fusion | flops 134217728 | bytes 8683520 | tf_op jit(solution)/shard_map/ntd,dkc->ntkc/dot_general | solution.py:524
  26.1 0.1 convert_reduce_fusion
  26.3 7.3 %collective-permute-done.6.refs_0_ = bf16[1168,256]{1,0:T(8,128)(2,1)S(1)} collective-permute-done((bf16[1168,256]{1,0:T(8,128)(2,1)S(1)}, bf16[1168,256]{1,0:T(8,128)(2,1)S(1)}, u32[]{:S(2)}, u32[]{:S(2)}) %collective-permute-start.6) | collective-permute-done | bytes 598048 | tf_op jit(solution)/shard_map/ppermute | solution.py:23
  33.7 0.6 copy-done.8
  34.3 0.6 collective-permute-start.8
  35.0 3.4 %collective-permute-start.10 = (bf16[6,2,128,256]{3,2,1,0:T(8,128)(2,1)}, bf16[6,2,128,256]{3,2,1,0:T(8,128)(2,1)}, u32[]{:S(2)}, u32[]{:S(2)}) collective-permute-start(bf16[6,2,128,256]{3,2,1,0:T(8,128)(2,1)} %get-tuple-element.98), channel_id=1, source_target_pairs={{0,8},{4,12},{8,0},{12,4},{1,9},{5,13},{9,1},{13,5},{2,10},{6,14},... | collective-permute-start | bytes 2359304 | tf_op jit(solution)/shard_map/ppermute | solution.py:23
  38.3 0.4 collective-permute-start.11
  38.7 22.6 %collective-permute-done.8.refs_1_ = bf16[1168,256]{1,0:T(8,128)(2,1)S(1)} collective-permute-done((bf16[1168,256]{1,0:T(8,128)(2,1)S(1)}, bf16[1168,256]{1,0:T(8,128)(2,1)S(1)}, u32[]{:S(2)}, u32[]{:S(2)}) %collective-permute-start.8) | collective-permute-done | bytes 598048 | tf_op jit(solution)/shard_map/ppermute | solution.py:23
  61.4 0.8 maximum_convert_fusion
  62.2 0.6 fusion.15
  62.8 45.7 %conditional.1 = (bf16[2,2048,256]{2,1,0:T(8,128)(2,1)}, bf16[8,2,512,256]{3,2,1,0:T(8,128)(2,1)}, bf16[4,2,2,2560]{3,2,1,0:T(2,128)(2,1)}, bf16[2,2,128,256]{3,2,1,0:T(8,128)(2,1)}) conditional(s32[]{:T(128)} %bitcast.14, () %tuple.16, (s32[]{:T(128)}, s32[1]{0:T(128)}, s32[2]{0:T(128)S(1)}, s32[2]{0:T(128)}, s32[32,256]{1,0:T(8,128)}, ...), branch_computations={%region_1.2_spmd, %region_2.3_spmd} | conditional | flops 401414 | bytes 12207067 | solution.py:614
  62.8 3.2 %adapt.1 = (bf16[2,2048,256]{2,1,0:T(8,128)(2,1)}, bf16[2,128,256]{2,1,0:T(8,128)(2,1)}, bf16[2,1024,256]{2,1,0:T(8,128)(2,1)}, bf16[2,128,256]{2,1,0:T(8,128)(2...) custom-call(s32[1]{0:T(128)} %get-tuple-element.43.me_ref.refs_0_, s32[2]{0:T(128)S(1)} %get-tuple-element.44.own_ref, ...), custom_call_target="tpu_custom_call" | custom-call | flops 1 | bytes 1 | tf_op jit(solution)/shard_map/cond/branch_1_fun/adapt/pallas_call | solution.py:313
  66.1 1.3 %collective-permute-start.1 = (bf16[2,128,256]{2,1,0:T(8,128)(2,1)}, bf16[2,128,256]{2,1,0:T(8,128)(2,1)S(1)}, u32[]{:S(2)}, u32[]{:S(2)}) collective-permute-start(bf16[2,128,256]{2,1,0:T(8,128)(2,1)} %get-tuple-element.55), channel_id=1, source_target_pairs={{0,16},{16,0},{1,17},{17,1},{2,18},{18,2},{3,19},{19,3},{4,20},{20... | collective-permute-start | bytes 393224 | tf_op jit(solution)/shard_map/cond/branch_1_fun/ppermute | solution.py:23
  67.4 0.8 collective-permute-start
  68.2 3.3 %collective-permute-done = f32[16,256]{1,0:T(8,128)S(1)} collective-permute-done((f32[16,256]{1,0:T(8,128)}, f32[16,256]{1,0:T(8,128)S(1)}, u32[]{:S(2)}, u32[]{:S(2)}) %collective-permute-start) | collective-permute-done | bytes 16416 | tf_op jit(solution)/shard_map/cond/branch_1_fun/ppermute | solution.py:23
  71.5 1.3 %add.35.refs_1_ = f32[16,256]{1,0:T(8,128)} add(f32[16,256]{1,0:T(8,128)} %get-tuple-element.53, f32[16,256]{1,0:T(8,128)S(1)} %collective-permute-done) | non-fusion elementwise | flops 4096 | bytes 49152 | tf_op jit(solution)/shard_map/cond/branch_1_fun/add | solution.py:579
  72.8 0.6 copy-done.2
  73.5 1.3 %collective-permute-start.2 = (bf16[2,1024,256]{2,1,0:T(8,128)(2,1)}, bf16[2,1024,256]{2,1,0:T(8,128)(2,1)S(1)}, u32[]{:S(2)}, u32[]{:S(2)}) collective-permute-start(bf16[2,1024,256]{2,1,0:T(8,128)(2,1)} %gate.7), channel_id=1, source_target_pairs={{0,16},{16,0},{1,17},{17,1},{2,18},{18,2},{3,19},{19,3},{4,20},{20... | collective-permute-start | bytes 3145736 | tf_op jit(solution)/shard_map/cond/branch_1_fun/ppermute | solution.py:23
  74.7 1.4 %collective-permute-done.3 = f32[16,256]{1,0:T(8,128)S(1)} collective-permute-done((f32[16,256]{1,0:T(8,128)}, f32[16,256]{1,0:T(8,128)S(1)}, u32[]{:S(2)}, u32[]{:S(2)}) %collective-permute-start.3) | collective-permute-done | bytes 16416 | tf_op jit(solution)/shard_map/cond/branch_1_fun/ppermute | solution.py:23
  76.1 0.7 add.36.low_ref
  76.8 1.5 %collective-permute-start.4 = (f32[16,256]{1,0:T(8,128)S(1)}, f32[16,256]{1,0:T(8,128)S(1)}, u32[]{:S(2)}, u32[]{:S(2)}) collective-permute-start(f32[16,256]{1,0:T(8,128)S(1)} %add.36.low_ref), channel_id=1, source_target_pairs={{0,2},{1,3},{2,0},{3,1},{4,6},{5,7},{6,4},{7,5},{8,10},{9,11},{10,... | collective-permute-start | bytes 49160 | tf_op jit(solution)/shard_map/cond/branch_1_fun/ppermute | solution.py:23
  78.3 2.2 %collective-permute-done.4.low_other_ref = f32[16,256]{1,0:T(8,128)S(1)} collective-permute-done((f32[16,256]{1,0:T(8,128)S(1)}, f32[16,256]{1,0:T(8,128)S(1)}, u32[]{:S(2)}, u32[]{:S(2)}) %collective-permute-start.4) | collective-permute-done | bytes 16416 | tf_op jit(solution)/shard_map/cond/branch_1_fun/ppermute | solution.py:23
  80.6 0.6 copy-done.13
  81.2 9.0 %attend.1.refs_4_ = bf16[8,2,2560]{2,1,0:T(2,128)(2,1)} custom-call(s32[8]{0:T(128)} %get-tuple-element.60.place_ref, s32[8]{0:T(128)} %get-tuple-element.61.count_ref, s32[8]{0:T(128)} %get-tuple-element.62.hot_ref, s32[1]{0:T(128)} %bitcast.group_ref, f32[16,256]{1,0:T(8,128)} %copy-done.10, f32[16,256]{1,0:T(8,128)} %copy-done.13, ...), custom_call_target="tpu_custom_call" | custom-call | flops 1 | bytes 1 | tf_op jit(solution)/shard_map/cond/branch_1_fun/attend/pallas_call | solution.py:431
  90.2 4.6 %all-to-all-start = ((bf16[4,2,2,2560]{3,2,1,0:T(2,128)(2,1)}), bf16[4,2,2,2560]{3,2,1,0:T(2,128)(2,1)}, u32[]{:S(2)}, u32[]{:S(2)}) async-start(bf16[4,2,2,2560]{3,2,1,0:T(2,128)(2,1)} %bitcast.32), calls=%async_computation | async-start | bytes 163840 | tf_op jit(solution)/shard_map/cond/branch_1_fun/all_to_all | solution.py:597
  94.8 3.1 %unpack.2.after_ref = bf16[8,2,512,256]{3,2,1,0:T(8,128)(2,1)} custom-call(s32[1]{0:T(128)} %get-tuple-element.43.me_ref.refs_0_, s32[4,8]{1,0:T(4,128)S(1)} %copy-done.12, s32[4,8]{1,0:T(4,128)S(1)} %get-tuple-element.58.refs_2_, bf16[8,2,512,256]{3,2,1,0:T(8,128)(2,1)} %get-tuple-element.59.cache_ref.refs_3_, bf16[8,2,2560]{2,1,0:T(2,128)(2,1)} %attend.1.refs_4_), custom_call_target="tpu_custom_call" | custom-call | flops 1 | bytes 1 | tf_op jit(solution)/shard_map/cond/branch_1_fun/unpack/pallas_call | solution.py:261
  98.0 0.7 copy.56
  98.7 1.0 copy-done.5
  99.7 2.2 %place_half.1 = bf16[2,2048,256]{2,1,0:T(8,128)(2,1)} custom-call(s32[1]{0:T(128)} %bitcast.group_ref, bf16[2,1024,256]{2,1,0:T(8,128)(2,1)} %copy-done.5, bf16[2,2048,256]{2,1,0:T(8,128)(2,1)} %get-tuple-element.56._, bf16[8,2,512,256]{3,2,1,0:T(8,128)(2,1)} %unpack.2.after_ref), custom_call_target="tpu_custom_call", output_to_operand_aliasing={{}: (2, {})} | custom-call | flops 1 | bytes 1 | tf_op jit(solution)/shard_map/cond/branch_1_fun/place_half/pallas_call | solution.py:340
  101.9 6.6 %all-to-all-done = bf16[4,2,2,2560]{3,2,1,0:T(2,128)(2,1)} async-done(((bf16[4,2,2,2560]{3,2,1,0:T(2,128)(2,1)}), bf16[4,2,2,2560]{3,2,1,0:T(2,128)(2,1)}, u32[]{:S(2)}, u32[]{:S(2)}) %all-to-all-start) | async-done | bytes 81952 | tf_op jit(solution)/shard_map/cond/branch_1_fun/all_to_all | solution.py:597
  108.5 3.7 %unpack.3 = (bf16[8,2,512,256]{3,2,1,0:T(8,128)(2,1)}, bf16[8,2,2048]{2,1,0:T(2,128)(2,1)}) custom-call(s32[1]{0:T(128)} %bitcast.4.me_ref.refs_0_, s32[4,8]{1,0:T(4,128)} %get-tuple-element.129.refs_1_, s32[4,8]{1,0:T(4,128)S(1)} %get-tuple-element.128.refs_2_, ...), custom_call_target="tpu_custom_call", output_to_operand_aliasing={{0}: (7, {})} | custom-call | flops 1 | bytes 1 | tf_op jit(solution)/shard_map/unpack/pallas_call | solution.py:261
  (81 shorter events, 1.2 us)
Async XLA Ops:
  0.6 2.4 %copy-start = (bf16[1,2048,256]{2,1,0:T(8,128)(2,1)S(1)}, bf16[1,2048,256]{2,1,0:T(8,128)(2,1)}, u32[]{:S(2)}) copy-start(bf16[1,2048,256]{2,1,0:T(8,128)(2,1)} %param.20) | copy-start | bytes 3145732
  0.6 20.3 %copy-start.6 = (bf16[8,2,8192]{2,1,0:T(2,128)(2,1)S(1)}, bf16[8,2,8192]{2,1,0:T(2,128)(2,1)}, u32[]{:S(2)}) copy-start(bf16[8,2,8192]{2,1,0:T(2,128)(2,1)} %param.12) | copy-start | bytes 786436
  0.7 18.4 %copy-start.16 = (s32[1,8]{1,0:T(1,128)S(1)}, s32[1,8]{1,0:T(1,128)}, u32[]{:S(2)}) copy-start(s32[1,8]{1,0:T(1,128)} %param.15) | copy-start | bytes 100
  1.4 12.1 %copy-start.17 = (s32[8]{0:T(128)}, s32[8]{0:T(128)S(1)}, u32[]{:S(2)}) copy-start(s32[8]{0:T(128)S(1)} %copy.88.dest_ref.refs_0_) | copy-start | bytes 100
  1.4 18.6 %copy-start.18 = (bf16[1,8]{1,0:T(2,128)(2,1)}, bf16[1,8]{1,0:T(2,128)(2,1)S(1)}, u32[]{:S(2)}) copy-start(bf16[1,8]{1,0:T(2,128)(2,1)S(1)} %convert_bitcast_fusion) | copy-start | bytes 52
  2.1 17.9 %copy-start.19 = (bf16[1,8]{1,0:T(2,128)(2,1)}, bf16[1,8]{1,0:T(2,128)(2,1)S(1)}, u32[]{:S(2)}) copy-start(bf16[1,8]{1,0:T(2,128)(2,1)S(1)} %convert.19) | copy-start | bytes 52
  3.1 30.5 %collective-permute-start.6 = (bf16[1168,256]{1,0:T(8,128)(2,1)S(1)}, bf16[1168,256]{1,0:T(8,128)(2,1)S(1)}, u32[]{:S(2)}, u32[]{:S(2)}) collective-permute-start(bf16[1168,256]{1,0:T(8,128)(2,1)S(1)} %pad_maximum_fusion), channel_id=1, source_target_pairs={{0,8},{4,12},{8,0},{12,4},{1,9},{5,13},{9,1},{13,5},{2,10},{6,14},... | collective-permute-start | bytes 1794056 | tf_op jit(solution)/shard_map/ppermute | solution.py:23
  7.2 27.7 %collective-permute-start.5 = (bf16[1168,256]{1,0:T(8,128)(2,1)S(1)}, bf16[1168,256]{1,0:T(8,128)(2,1)S(1)}, u32[]{:S(2)}, u32[]{:S(2)}) collective-permute-start(bf16[1168,256]{1,0:T(8,128)(2,1)S(1)} %pad_maximum_fusion), channel_id=1, source_target_pairs={{0,4},{4,0},{8,12},{12,8},{1,5},{5,1},{9,13},{13,9},{2,6},{6,2},{1... | collective-permute-start | bytes 1794056 | tf_op jit(solution)/shard_map/ppermute | solution.py:23
  17.6 8.4 %collective-permute-start.7 = (bf16[16,1152]{1,0:T(8,128)(2,1)}, bf16[16,1152]{1,0:T(8,128)(2,1)S(1)}, u32[]{:S(2)}, u32[]{:S(2)}) collective-permute-start(bf16[16,1152]{1,0:T(8,128)(2,1)} %gate.8), channel_id=1, source_target_pairs={{0,16},{16,0},{1,17},{17,1},{2,18},{18,2},{3,19},{19,3},{4,20},{20... | collective-permute-start | bytes 110600 | tf_op jit(solution)/shard_map/ppermute | solution.py:23
  20.9 5.0 %copy-start.11 = (bf16[8,2,2048]{2,1,0:T(2,128)(2,1)S(1)}, bf16[8,2,2048]{2,1,0:T(2,128)(2,1)}, u32[]{:S(2)}) copy-start(bf16[8,2,2048]{2,1,0:T(2,128)(2,1)} %param.13) | copy-start | bytes 196612
  25.6 37.3 %copy-start.1 = (s32[2]{0:T(128)S(1)}, s32[2]{0:T(128)}, u32[]{:S(2)}) copy-start(s32[2]{0:T(128)} %param.18) | copy-start | bytes 28
  26.1 7.6 %copy-start.4 = (bf16[8,2,16,128]{3,2,1,0:T(8,128)(2,1)}, bf16[8,2,16,128]{3,2,1,0:T(8,128)(2,1)S(1)}, u32[]{:S(2)}) copy-start(bf16[8,2,16,128]{3,2,1,0:T(8,128)(2,1)S(1)} %get-tuple-element.91.refs_5_) | copy-start | bytes 196612
  26.1 7.6 %copy-start.9 = (f32[8,2,128]{2,1,0:T(2,128)}, f32[8,2,128]{2,1,0:T(2,128)S(1)}, u32[]{:S(2)}) copy-start(f32[8,2,128]{2,1,0:T(2,128)S(1)} %get-tuple-element.94.refs_8_) | copy-start | bytes 24580
  26.1 7.6 %copy-start.14 = (s32[8]{0:T(128)}, s32[8]{0:T(128)S(1)}, u32[]{:S(2)}) copy-start(s32[8]{0:T(128)S(1)} %get-tuple-element.90.refs_4_) | copy-start | bytes 100
  26.1 7.7 %copy-start.15 = (s32[2]{0:T(128)}, s32[2]{0:T(128)S(1)}, u32[]{:S(2)}) copy-start(s32[2]{0:T(128)S(1)} %get-tuple-element.92.refs_6_) | copy-start | bytes 28
  33.7 0.6 copy-start.8
  34.3 27.0 %collective-permute-start.8 = (bf16[1168,256]{1,0:T(8,128)(2,1)S(1)}, bf16[1168,256]{1,0:T(8,128)(2,1)S(1)}, u32[]{:S(2)}, u32[]{:S(2)}) collective-permute-start(bf16[1168,256]{1,0:T(8,128)(2,1)S(1)} %gate.11.refs_2_), channel_id=1, source_target_pairs={{0,4},{4,0},{8,12},{12,8},{1,5},{5,1},{9,13},{13,9},{2,6},{6,2},{1... | collective-permute-start | bytes 1794056 | tf_op jit(solution)/shard_map/ppermute | solution.py:23
  35.0 73.5 %collective-permute-start.10 = (bf16[6,2,128,256]{3,2,1,0:T(8,128)(2,1)}, bf16[6,2,128,256]{3,2,1,0:T(8,128)(2,1)}, u32[]{:S(2)}, u32[]{:S(2)}) collective-permute-start(bf16[6,2,128,256]{3,2,1,0:T(8,128)(2,1)} %get-tuple-element.98), channel_id=1, source_target_pairs={{0,8},{4,12},{8,0},{12,4},{1,9},{5,13},{9,1},{13,5},{2,10},{6,14},... | collective-permute-start | bytes 2359304 | tf_op jit(solution)/shard_map/ppermute | solution.py:23
  38.3 70.2 %collective-permute-start.11 = (bf16[6,2,128,256]{3,2,1,0:T(8,128)(2,1)}, bf16[6,2,128,256]{3,2,1,0:T(8,128)(2,1)}, u32[]{:S(2)}, u32[]{:S(2)}) collective-permute-start(bf16[6,2,128,256]{3,2,1,0:T(8,128)(2,1)} %get-tuple-element.99), channel_id=1, source_target_pairs={{0,12},{4,8},{8,4},{12,0},{1,13},{5,9},{9,5},{13,1},{2,14},{6,10},... | collective-permute-start | bytes 2359304 | tf_op jit(solution)/shard_map/ppermute | solution.py:23
  61.3 47.2 %collective-permute-start.9 = (bf16[6,2,128,256]{3,2,1,0:T(8,128)(2,1)}, bf16[6,2,128,256]{3,2,1,0:T(8,128)(2,1)}, u32[]{:S(2)}, u32[]{:S(2)}) collective-permute-start(bf16[6,2,128,256]{3,2,1,0:T(8,128)(2,1)} %gate.12), channel_id=1, source_target_pairs={{0,4},{4,0},{8,12},{12,8},{1,5},{5,1},{9,13},{13,9},{2,6},{6,2},{1... | collective-permute-start | bytes 2359304 | tf_op jit(solution)/shard_map/ppermute | solution.py:23
  66.1 28.7 %copy-start.12 = (s32[4,8]{1,0:T(4,128)S(1)}, s32[4,8]{1,0:T(4,128)}, u32[]{:S(2)}) copy-start(s32[4,8]{1,0:T(4,128)} %get-tuple-element.57.refs_1_) | copy-start | bytes 388 | tf_op jit(solution)/shard_map/cond
  66.1 6.7 %collective-permute-start.1 = (bf16[2,128,256]{2,1,0:T(8,128)(2,1)}, bf16[2,128,256]{2,1,0:T(8,128)(2,1)S(1)}, u32[]{:S(2)}, u32[]{:S(2)}) collective-permute-start(bf16[2,128,256]{2,1,0:T(8,128)(2,1)} %get-tuple-element.55), channel_id=1, source_target_pairs={{0,16},{16,0},{1,17},{17,1},{2,18},{18,2},{3,19},{19,3},{4,20},{20... | collective-permute-start | bytes 393224 | tf_op jit(solution)/shard_map/cond/branch_1_fun/ppermute | solution.py:23
  67.4 4.1 %collective-permute-start = (f32[16,256]{1,0:T(8,128)}, f32[16,256]{1,0:T(8,128)S(1)}, u32[]{:S(2)}, u32[]{:S(2)}) collective-permute-start(f32[16,256]{1,0:T(8,128)} %get-tuple-element.54), channel_id=1, source_target_pairs={{0,16},{16,0},{1,17},{17,1},{2,18},{18,2},{3,19},{19,3},{4,20},{20... | collective-permute-start | bytes 49160 | tf_op jit(solution)/shard_map/cond/branch_1_fun/ppermute | solution.py:23
  72.8 0.7 copy-start.2
  73.5 25.2 %collective-permute-start.2 = (bf16[2,1024,256]{2,1,0:T(8,128)(2,1)}, bf16[2,1024,256]{2,1,0:T(8,128)(2,1)S(1)}, u32[]{:S(2)}, u32[]{:S(2)}) collective-permute-start(bf16[2,1024,256]{2,1,0:T(8,128)(2,1)} %gate.7), channel_id=1, source_target_pairs={{0,16},{16,0},{1,17},{17,1},{2,18},{18,2},{3,19},{19,3},{4,20},{20... | collective-permute-start | bytes 3145736 | tf_op jit(solution)/shard_map/cond/branch_1_fun/ppermute | solution.py:23
  74.7 1.4 %collective-permute-start.3 = (f32[16,256]{1,0:T(8,128)}, f32[16,256]{1,0:T(8,128)S(1)}, u32[]{:S(2)}, u32[]{:S(2)}) collective-permute-start(f32[16,256]{1,0:T(8,128)} %add.35.refs_1_), channel_id=1, source_target_pairs={{0,1},{1,0},{2,3},{3,2},{4,5},{5,4},{6,7},{7,6},{8,9},{9,8},{10,11... | collective-permute-start | bytes 49160 | tf_op jit(solution)/shard_map/cond/branch_1_fun/ppermute | solution.py:23
  76.8 3.7 %copy-start.10 = (f32[16,256]{1,0:T(8,128)}, f32[16,256]{1,0:T(8,128)S(1)}, u32[]{:S(2)}) copy-start(f32[16,256]{1,0:T(8,128)S(1)} %add.36.low_ref) | copy-start | bytes 49156 | tf_op jit(solution)/shard_map/cond
  76.8 3.7 %collective-permute-start.4 = (f32[16,256]{1,0:T(8,128)S(1)}, f32[16,256]{1,0:T(8,128)S(1)}, u32[]{:S(2)}, u32[]{:S(2)}) collective-permute-start(f32[16,256]{1,0:T(8,128)S(1)} %add.36.low_ref), channel_id=1, source_target_pairs={{0,2},{1,3},{2,0},{3,1},{4,6},{5,7},{6,4},{7,5},{8,10},{9,11},{10,... | collective-permute-start | bytes 49160 | tf_op jit(solution)/shard_map/cond/branch_1_fun/ppermute | solution.py:23
  80.6 0.6 copy-start.13
  90.2 18.3 %all-to-all-start = ((bf16[4,2,2,2560]{3,2,1,0:T(2,128)(2,1)}), bf16[4,2,2,2560]{3,2,1,0:T(2,128)(2,1)}, u32[]{:S(2)}, u32[]{:S(2)}) async-start(bf16[4,2,2,2560]{3,2,1,0:T(2,128)(2,1)} %bitcast.32), calls=%async_computation | async-start | bytes 163840 | tf_op jit(solution)/shard_map/cond/branch_1_fun/all_to_all | solution.py:597
  94.8 3.1 %copy-start.3 = (bf16[2,128,256]{2,1,0:T(8,128)(2,1)S(1)}, bf16[2,128,256]{2,1,0:T(8,128)(2,1)}, u32[]{:S(2)}) copy-start(bf16[2,128,256]{2,1,0:T(8,128)(2,1)} %copy-done.2) | copy-start | bytes 393220 | tf_op jit(solution)/shard_map/cond
  94.8 3.1 %copy-start.7 = (bf16[2,128,256]{2,1,0:T(8,128)(2,1)S(1)}, bf16[2,128,256]{2,1,0:T(8,128)(2,1)}, u32[]{:S(2)}) copy-start(bf16[2,128,256]{2,1,0:T(8,128)(2,1)} %get-tuple-element.63.ours_ref) | copy-start | bytes 393220 | tf_op jit(solution)/shard_map/cond
  98.7 1.0 copy-start.5

commit v3 on v2

--- a/solution.py
+++ b/solution.py
@@ -265,7 +265,7 @@
         out_specs=out_specs,
         scratch_shapes=[pltpu.SemaphoreType.DMA((amount,))] + scratch,
         input_output_aliases=aliases,
-        compiler_params=pltpu.CompilerParams(vmem_limit_bytes=60 << 20),
+        compiler_params=pltpu.CompilerParams(vmem_limit_bytes=8 << 20),
         cost_estimate=CHEAP,
         name="unpack",
     )(*args)
@@ -343,7 +343,7 @@
         in_specs=[SMEM, VMEM, HBM, HBM],
         out_specs=HBM,
         scratch_shapes=[pltpu.SemaphoreType.DMA],
-        compiler_params=pltpu.CompilerParams(vmem_limit_bytes=60 << 20),
+        compiler_params=pltpu.CompilerParams(vmem_limit_bytes=8 << 20),
         input_output_aliases={2: 0},
         cost_estimate=CHEAP,
         name="place_half",

time: 113 us -> 113 us (level)
    all_to_all x1, waiting for transfers between devices: 6.63 us -> 8.91 us  [serve(): lax.all_to_all(small.reshape((replicas, pairs) + small.shape[1:]), 'repli...]
    ppermute x12, waiting for transfers between devices: 36.9 us -> 35.4 us  [exchange(): return lax.ppermute(values, axis, [(i, i ^ mask) for i in range(size)])]
    slice x3, local copies, waits for them, and re-layouts: 0.01 us -> 1.37 us  [per_device(): p[half + extra, :2 * requests]]
    pallas_call x1, Pallas kernels: 2.2 us -> 0.98 us  [place_half(): pl.pallas_call(place_kernel, out_shape=jax.ShapeDtypeStruct(out.shape, ou...]
    cond x15 -> x13, local copies, waits for them, and re-layouts: 2.96 us -> 2.9 us
where the time goes in v3:
time: 113 us; the launch traced here: 112 us
  waiting for transfers between devices  44.3 us (39%)
  Pallas kernels  24.3 us (22%)
  starting transfers between devices  20.9 us (18%)
  local copies, waits for them, and re-layouts  9.89 us (9%)
  other arithmetic  7.17 us (6%)
  matrix products  4.65 us (4%)
    ppermute x12, waiting for transfers between devices, exchange(): return lax.ppermute(values, axis, [(i, i ^ mask) for i in range(size)])  35.4 us
    ppermute x12, starting transfers between devices, exchange(): return lax.ppermute(values, axis, [(i, i ^ mask) for i in range(size)])  16.4 us
    all_to_all x1, waiting for transfers between devices, serve(): lax.all_to_all(small.reshape((replicas, pairs) + small.shape[1:]), 'repli...  8.91 us
    pallas_call x1, Pallas kernels, attend(): pl.pallas_call(attend_kernel, out_shape=jax.ShapeDtypeStruct((slots, 2, (...  8.84 us
    pallas_call x2, Pallas kernels, unpack(): pl.pallas_call(functools.partial(unpack_kernel, layout, own, fill, tail,...  6.8 us
    dot_general x1, matrix products, per_device(): jnp.einsum('ntd,dkc->ntkc', hidden, base_key_value_weight, preferred_elem...  4.65 us
    all_to_all x1, starting transfers between devices, serve(): lax.all_to_all(small.reshape((replicas, pairs) + small.shape[1:]), 'repli...  4.54 us
    pallas_call x1, Pallas kernels, pack(): pl.pallas_call(functools.partial(pack_kernel, layout, live), out_shape=[j...  4.01 us
  transfers between devices with their start and end apart: 13, of which 6 were waited for; matrix products, arithmetic and copies ran while one was open for 14% of the time, Pallas kernels for 19%

profile of v3, /device:TPU:0, one launch (start us, length us, event | category | flops | bytes accessed | tf_op | source)
XLA Modules:
  0.0 112.2 jit_solution(16946322953614140737)
XLA Ops:
  0.7 0.8 copy.88.dest_ref.refs_0_
  1.4 0.7 convert.19
  2.2 0.8 dynamic-slice_bitcast_fusion.1
  3.1 4.1 %collective-permute-start.6 = (bf16[1168,256]{1,0:T(8,128)(2,1)S(1)}, bf16[1168,256]{1,0:T(8,128)(2,1)S(1)}, u32[]{:S(2)}, u32[]{:S(2)}) collective-permute-start(bf16[1168,256]{1,0:T(8,128)(2,1)S(1)} %pad_maximum_fusion), channel_id=1, source_target_pairs={{0,8},{4,12},{8,0},{12,4},{1,9},{5,13},{9,1},{13,5},{2,10},{6,14},... | collective-permute-start | bytes 1794056 | tf_op jit(solution)/shard_map/ppermute | solution.py:23
  7.2 1.6 %collective-permute-start.5 = (bf16[1168,256]{1,0:T(8,128)(2,1)S(1)}, bf16[1168,256]{1,0:T(8,128)(2,1)S(1)}, u32[]{:S(2)}, u32[]{:S(2)}) collective-permute-start(bf16[1168,256]{1,0:T(8,128)(2,1)S(1)} %pad_maximum_fusion), channel_id=1, source_target_pairs={{0,4},{4,0},{8,12},{12,8},{1,5},{5,1},{9,13},{13,9},{2,6},{6,2},{1... | collective-permute-start | bytes 1794056 | tf_op jit(solution)/shard_map/ppermute | solution.py:23
  8.8 0.7 compare_select_fusion
  9.4 0.7 convert.22
  10.1 1.3 %gather_fusion = s32[8]{0:T(128)S(1)} fusion(s32[2]{0:T(128)} %param.18, s32[1024]{0:T(1024)S(1)} %pad_clamp_fusion), kind=kCustom, calls=%fused_computation | custom fusion | bytes 96 | tf_op jit(solution)/shard_map/gather | solution.py:509
  11.5 0.1 broadcast_in_dim_reshape.4
  11.7 0.1 copy.46
  11.8 1.1 reshape.106
  12.9 0.6 fusion.5.refs_0_
  13.5 4.0 %pack.1 = (bf16[6,2,128,256]{3,2,1,0:T(8,128)(2,1)}, bf16[6,2,128,256]{3,2,1,0:T(8,128)(2,1)}, bf16[6,2,128,256]{3,2,1,0:T(8,128)(2,1)}, f32[8,128]{1,0:T(8,128)}) custom-call(s32[1]{0:T(128)} %bitcast.4.me_ref.refs_0_, s32[8]{0:T(128)} %copy-done.12, s32[8]{0:T(128)} %bitcast.34, bf16[8,2,512,256]{3,2,1,0:T(8,128)(2,1)} %cache_ref.1), custom_call_target="tpu_custom_call" | custom-call | flops 1 | bytes 1 | tf_op jit(solution)/shard_map/pack/pallas_call | solution.py:88
  17.6 1.5 %collective-permute-start.7 = (bf16[16,1152]{1,0:T(8,128)(2,1)}, bf16[16,1152]{1,0:T(8,128)(2,1)S(1)}, u32[]{:S(2)}, u32[]{:S(2)}) collective-permute-start(bf16[16,1152]{1,0:T(8,128)(2,1)} %gate.8), channel_id=1, source_target_pairs={{0,16},{16,0},{1,17},{17,1},{2,18},{18,2},{3,19},{19,3},{4,20},{20... | collective-permute-start | bytes 110600 | tf_op jit(solution)/shard_map/ppermute | solution.py:23
  19.1 0.9 convert_reduce_fusion.1
  20.1 0.7 multiply_add_fusion.refs_0_
  20.7 0.2 fusion.14
  20.9 4.7 %fusion = f32[8,2,2,256]{3,0,2,1:T(8,128)S(1)} fusion(bf16[8192,2,256]{2,1,0:T(2,128)(2,1)} %param.19, bf16[8,2,8192,1]{2,1,0,3:T(2,128)(2,1)S(1)} %bitcast.32), kind=kOutput, calls=%fused_computation.2 | convolution fusion | flops 134217728 | bytes 8683520 | tf_op jit(solution)/shard_map/ntd,dkc->ntkc/dot_general | solution.py:524
  26.1 0.1 convert_reduce_fusion
  26.3 7.4 %collective-permute-done.6.refs_0_ = bf16[1168,256]{1,0:T(8,128)(2,1)S(1)} collective-permute-done((bf16[1168,256]{1,0:T(8,128)(2,1)S(1)}, bf16[1168,256]{1,0:T(8,128)(2,1)S(1)}, u32[]{:S(2)}, u32[]{:S(2)}) %collective-permute-start.6) | collective-permute-done | bytes 598048 | tf_op jit(solution)/shard_map/ppermute | solution.py:23
  33.7 0.6 collective-permute-start.8
  34.3 0.8 copy-done.3
  35.2 3.4 %collective-permute-start.10 = (bf16[6,2,128,256]{3,2,1,0:T(8,128)(2,1)}, bf16[6,2,128,256]{3,2,1,0:T(8,128)(2,1)S(1)}, u32[]{:S(2)}, u32[]{:S(2)}) collective-permute-start(bf16[6,2,128,256]{3,2,1,0:T(8,128)(2,1)} %get-tuple-element.98), channel_id=1, source_target_pairs={{0,8},{4,12},{8,0},{12,4},{1,9},{5,13},{9,1},{13,5},{2,10},{6,14},... | collective-permute-start | bytes 2359304 | tf_op jit(solution)/shard_map/ppermute | solution.py:23
  38.5 0.4 collective-permute-start.11
  38.9 21.1 %collective-permute-done.8.refs_1_ = bf16[1168,256]{1,0:T(8,128)(2,1)} collective-permute-done((bf16[1168,256]{1,0:T(8,128)(2,1)S(1)}, bf16[1168,256]{1,0:T(8,128)(2,1)}, u32[]{:S(2)}, u32[]{:S(2)}) %collective-permute-start.8) | collective-permute-done | bytes 598048 | tf_op jit(solution)/shard_map/ppermute | solution.py:23
  60.1 0.7 slice.40
  60.7 0.7 slice.45
  61.6 47.1 %conditional.1 = (bf16[2,2048,256]{2,1,0:T(8,128)(2,1)}, bf16[8,2,512,256]{3,2,1,0:T(8,128)(2,1)}, bf16[4,2,2,2560]{3,2,1,0:T(2,128)(2,1)}, bf16[2,2,128,256]{3,2,1,0:T(8,128)(2,1)}) conditional(s32[]{:T(128)} %bitcast.14, () %tuple.16, (s32[]{:T(128)}, s32[1]{0:T(128)}, s32[2]{0:T(128)S(1)}, s32[2]{0:T(128)S(1)}, s32[32,256]{1,0:T(8,128)S(1)}, ...), branch_computations={%region_1.2_spmd, %region_2.3_spmd} | conditional | flops 401414 | bytes 8339903 | solution.py:614
  61.6 3.7 %adapt.1 = (bf16[2,2048,256]{2,1,0:T(8,128)(2,1)}, bf16[2,128,256]{2,1,0:T(8,128)(2,1)}, bf16[2,1024,256]{2,1,0:T(8,128)(2,1)}, bf16[2,128,256]{2,1,0:T(8,128)(2...) custom-call(s32[1]{0:T(128)} %get-tuple-element.43.me_ref.refs_0_, s32[2]{0:T(128)S(1)} %get-tuple-element.44.own_ref, ...), custom_call_target="tpu_custom_call" | custom-call | flops 1 | bytes 1 | tf_op jit(solution)/shard_map/cond/branch_1_fun/adapt/pallas_call | solution.py:313
  65.3 1.4 %collective-permute-start.1 = (bf16[2,128,256]{2,1,0:T(8,128)(2,1)}, bf16[2,128,256]{2,1,0:T(8,128)(2,1)S(1)}, u32[]{:S(2)}, u32[]{:S(2)}) collective-permute-start(bf16[2,128,256]{2,1,0:T(8,128)(2,1)} %get-tuple-element.55), channel_id=1, source_target_pairs={{0,16},{16,0},{1,17},{17,1},{2,18},{18,2},{3,19},{19,3},{4,20},{20... | collective-permute-start | bytes 393224 | tf_op jit(solution)/shard_map/cond/branch_1_fun/ppermute | solution.py:23
  66.6 0.7 collective-permute-start
  67.4 3.3 %collective-permute-done = f32[16,256]{1,0:T(8,128)S(1)} collective-permute-done((f32[16,256]{1,0:T(8,128)}, f32[16,256]{1,0:T(8,128)S(1)}, u32[]{:S(2)}, u32[]{:S(2)}) %collective-permute-start) | collective-permute-done | bytes 16416 | tf_op jit(solution)/shard_map/cond/branch_1_fun/ppermute | solution.py:23
  70.7 1.3 %add.35.refs_1_ = f32[16,256]{1,0:T(8,128)} add(f32[16,256]{1,0:T(8,128)} %get-tuple-element.53, f32[16,256]{1,0:T(8,128)S(1)} %collective-permute-done) | non-fusion elementwise | flops 4096 | bytes 49152 | tf_op jit(solution)/shard_map/cond/branch_1_fun/add | solution.py:579
  72.0 0.6 copy-done.4
  72.7 1.3 %collective-permute-start.2 = (bf16[2,1024,256]{2,1,0:T(8,128)(2,1)}, bf16[2,1024,256]{2,1,0:T(8,128)(2,1)S(1)}, u32[]{:S(2)}, u32[]{:S(2)}) collective-permute-start(bf16[2,1024,256]{2,1,0:T(8,128)(2,1)} %gate.7), channel_id=1, source_target_pairs={{0,16},{16,0},{1,17},{17,1},{2,18},{18,2},{3,19},{19,3},{4,20},{20... | collective-permute-start | bytes 3145736 | tf_op jit(solution)/shard_map/cond/branch_1_fun/ppermute | solution.py:23
  74.0 1.4 %collective-permute-done.3 = f32[16,256]{1,0:T(8,128)S(1)} collective-permute-done((f32[16,256]{1,0:T(8,128)}, f32[16,256]{1,0:T(8,128)S(1)}, u32[]{:S(2)}, u32[]{:S(2)}) %collective-permute-start.3) | collective-permute-done | bytes 16416 | tf_op jit(solution)/shard_map/cond/branch_1_fun/ppermute | solution.py:23
  75.4 0.7 add.36.low_ref
  76.1 1.5 %collective-permute-start.4 = (f32[16,256]{1,0:T(8,128)S(1)}, f32[16,256]{1,0:T(8,128)S(1)}, u32[]{:S(2)}, u32[]{:S(2)}) collective-permute-start(f32[16,256]{1,0:T(8,128)S(1)} %add.36.low_ref), channel_id=1, source_target_pairs={{0,2},{1,3},{2,0},{3,1},{4,6},{5,7},{6,4},{7,5},{8,10},{9,11},{10,... | collective-permute-start | bytes 49160 | tf_op jit(solution)/shard_map/cond/branch_1_fun/ppermute | solution.py:23
  77.6 2.2 %collective-permute-done.4.low_other_ref = f32[16,256]{1,0:T(8,128)S(1)} collective-permute-done((f32[16,256]{1,0:T(8,128)S(1)}, f32[16,256]{1,0:T(8,128)S(1)}, u32[]{:S(2)}, u32[]{:S(2)}) %collective-permute-start.4) | collective-permute-done | bytes 16416 | tf_op jit(solution)/shard_map/cond/branch_1_fun/ppermute | solution.py:23
  79.8 0.6 copy-done.10
  80.4 8.8 %attend.1.refs_4_ = bf16[8,2,2560]{2,1,0:T(2,128)(2,1)} custom-call(s32[8]{0:T(128)S(1)} %get-tuple-element.60.place_ref, s32[8]{0:T(128)S(1)} %get-tuple-element.61.count_ref, s32[8]{0:T(128)S(1)} %get-tuple-element.62.hot_ref, s32[1]{0:T(128)} %bitcast.group_ref, f32[16,256]{1,0:T(8,128)} %copy-done.8, f32[16,256]{1,0:T(8,128)} %copy-done.10, ...), custom_call_target="tpu_custom_call" | custom-call | flops 1 | bytes 1 | tf_op jit(solution)/shard_map/cond/branch_1_fun/attend/pallas_call | solution.py:431
  89.3 4.5 %all-to-all-start = ((bf16[4,2,2,2560]{3,2,1,0:T(2,128)(2,1)}), bf16[4,2,2,2560]{3,2,1,0:T(2,128)(2,1)}, u32[]{:S(2)}, u32[]{:S(2)}) async-start(bf16[4,2,2,2560]{3,2,1,0:T(2,128)(2,1)} %bitcast.29), calls=%async_computation | async-start | bytes 163840 | tf_op jit(solution)/shard_map/cond/branch_1_fun/all_to_all | solution.py:597
  93.8 0.9 copy-done.1
  94.7 3.3 %unpack.2.after_ref = bf16[8,2,512,256]{3,2,1,0:T(8,128)(2,1)} custom-call(s32[1]{0:T(128)} %get-tuple-element.43.me_ref.refs_0_, s32[4,8]{1,0:T(4,128)S(1)} %get-tuple-element.57.refs_1_, s32[4,8]{1,0:T(4,128)S(1)} %get-tuple-element.58.refs_2_, bf16[8,2,512,256]{3,2,1,0:T(8,128)(2,1)} %get-tuple-element.59.cache_ref.refs_3_, bf16[8,2,2560]{2,1,0:T(2,128)(2,1)S(1)} %copy-done.1), custom_call_target="tpu_custom_call" | custom-call | flops 1 | bytes 1 | tf_op jit(solution)/shard_map/cond/branch_1_fun/unpack/pallas_call | solution.py:261
  98.1 0.7 copy.56
  98.8 1.0 place_half.1
  99.8 8.9 %all-to-all-done = bf16[4,2,2,2560]{3,2,1,0:T(2,128)(2,1)} async-done(((bf16[4,2,2,2560]{3,2,1,0:T(2,128)(2,1)}), bf16[4,2,2,2560]{3,2,1,0:T(2,128)(2,1)}, u32[]{:S(2)}, u32[]{:S(2)}) %all-to-all-start) | async-done | bytes 81952 | tf_op jit(solution)/shard_map/cond/branch_1_fun/all_to_all | solution.py:597
  108.7 3.5 %unpack.3 = (bf16[8,2,512,256]{3,2,1,0:T(8,128)(2,1)}, bf16[8,2,2048]{2,1,0:T(2,128)(2,1)}) custom-call(s32[1]{0:T(128)} %bitcast.4.me_ref.refs_0_, s32[4,8]{1,0:T(4,128)S(1)} %get-tuple-element.129.refs_1_, s32[4,8]{1,0:T(4,128)S(1)} %get-tuple-element.128.refs_2_, ...), custom_call_target="tpu_custom_call", output_to_operand_aliasing={{0}: (7, {})} | custom-call | flops 1 | bytes 1 | tf_op jit(solution)/shard_map/unpack/pallas_call | solution.py:261
  (69 shorter events, 1.4 us)
Async XLA Ops:
  0.6 2.4 %copy-start = (bf16[1,2048,256]{2,1,0:T(8,128)(2,1)S(1)}, bf16[1,2048,256]{2,1,0:T(8,128)(2,1)}, u32[]{:S(2)}) copy-start(bf16[1,2048,256]{2,1,0:T(8,128)(2,1)} %param.20) | copy-start | bytes 3145732
  0.6 20.3 %copy-start.6 = (bf16[8,2,8192]{2,1,0:T(2,128)(2,1)S(1)}, bf16[8,2,8192]{2,1,0:T(2,128)(2,1)}, u32[]{:S(2)}) copy-start(bf16[8,2,8192]{2,1,0:T(2,128)(2,1)} %param.12) | copy-start | bytes 786436
  0.7 18.4 %copy-start.11 = (s32[1,8]{1,0:T(1,128)S(1)}, s32[1,8]{1,0:T(1,128)}, u32[]{:S(2)}) copy-start(s32[1,8]{1,0:T(1,128)} %param.15) | copy-start | bytes 100
  1.4 12.1 %copy-start.12 = (s32[8]{0:T(128)}, s32[8]{0:T(128)S(1)}, u32[]{:S(2)}) copy-start(s32[8]{0:T(128)S(1)} %copy.88.dest_ref.refs_0_) | copy-start | bytes 100
  3.1 30.5 %collective-permute-start.6 = (bf16[1168,256]{1,0:T(8,128)(2,1)S(1)}, bf16[1168,256]{1,0:T(8,128)(2,1)S(1)}, u32[]{:S(2)}, u32[]{:S(2)}) collective-permute-start(bf16[1168,256]{1,0:T(8,128)(2,1)S(1)} %pad_maximum_fusion), channel_id=1, source_target_pairs={{0,8},{4,12},{8,0},{12,4},{1,9},{5,13},{9,1},{13,5},{2,10},{6,14},... | collective-permute-start | bytes 1794056 | tf_op jit(solution)/shard_map/ppermute | solution.py:23
  7.2 27.1 %collective-permute-start.5 = (bf16[1168,256]{1,0:T(8,128)(2,1)S(1)}, bf16[1168,256]{1,0:T(8,128)(2,1)S(1)}, u32[]{:S(2)}, u32[]{:S(2)}) collective-permute-start(bf16[1168,256]{1,0:T(8,128)(2,1)S(1)} %pad_maximum_fusion), channel_id=1, source_target_pairs={{0,4},{4,0},{8,12},{12,8},{1,5},{5,1},{9,13},{13,9},{2,6},{6,2},{1... | collective-permute-start | bytes 1794056 | tf_op jit(solution)/shard_map/ppermute | solution.py:23
  17.6 8.4 %collective-permute-start.7 = (bf16[16,1152]{1,0:T(8,128)(2,1)}, bf16[16,1152]{1,0:T(8,128)(2,1)S(1)}, u32[]{:S(2)}, u32[]{:S(2)}) collective-permute-start(bf16[16,1152]{1,0:T(8,128)(2,1)} %gate.8), channel_id=1, source_target_pairs={{0,16},{16,0},{1,17},{17,1},{2,18},{18,2},{3,19},{19,3},{4,20},{20... | collective-permute-start | bytes 110600 | tf_op jit(solution)/shard_map/ppermute | solution.py:23
  20.9 5.0 %copy-start.9 = (bf16[8,2,2048]{2,1,0:T(2,128)(2,1)S(1)}, bf16[8,2,2048]{2,1,0:T(2,128)(2,1)}, u32[]{:S(2)}) copy-start(bf16[8,2,2048]{2,1,0:T(2,128)(2,1)} %param.13) | copy-start | bytes 196612
  25.6 36.0 %copy-start.2 = (s32[2]{0:T(128)S(1)}, s32[2]{0:T(128)}, u32[]{:S(2)}) copy-start(s32[2]{0:T(128)} %param.18) | copy-start | bytes 28
  25.6 36.0 %copy-start.13 = (s32[8]{0:T(128)S(1)}, s32[8]{0:T(128)}, u32[]{:S(2)}) copy-start(s32[8]{0:T(128)} %param.16) | copy-start | bytes 100
  33.7 26.3 %collective-permute-start.8 = (bf16[1168,256]{1,0:T(8,128)(2,1)S(1)}, bf16[1168,256]{1,0:T(8,128)(2,1)}, u32[]{:S(2)}, u32[]{:S(2)}) collective-permute-start(bf16[1168,256]{1,0:T(8,128)(2,1)S(1)} %gate.11.refs_2_), channel_id=1, source_target_pairs={{0,4},{4,0},{8,12},{12,8},{1,5},{5,1},{9,13},{13,9},{2,6},{6,2},{1... | collective-permute-start | bytes 1794056 | tf_op jit(solution)/shard_map/ppermute | solution.py:23
  34.3 0.8 copy-start.3
  35.2 73.5 %collective-permute-start.10 = (bf16[6,2,128,256]{3,2,1,0:T(8,128)(2,1)}, bf16[6,2,128,256]{3,2,1,0:T(8,128)(2,1)S(1)}, u32[]{:S(2)}, u32[]{:S(2)}) collective-permute-start(bf16[6,2,128,256]{3,2,1,0:T(8,128)(2,1)} %get-tuple-element.98), channel_id=1, source_target_pairs={{0,8},{4,12},{8,0},{12,4},{1,9},{5,13},{9,1},{13,5},{2,10},{6,14},... | collective-permute-start | bytes 2359304 | tf_op jit(solution)/shard_map/ppermute | solution.py:23
  38.5 70.2 %collective-permute-start.11 = (bf16[6,2,128,256]{3,2,1,0:T(8,128)(2,1)}, bf16[6,2,128,256]{3,2,1,0:T(8,128)(2,1)}, u32[]{:S(2)}, u32[]{:S(2)}) collective-permute-start(bf16[6,2,128,256]{3,2,1,0:T(8,128)(2,1)} %get-tuple-element.99), channel_id=1, source_target_pairs={{0,12},{4,8},{8,4},{12,0},{1,13},{5,9},{9,5},{13,1},{2,14},{6,10},... | collective-permute-start | bytes 2359304 | tf_op jit(solution)/shard_map/ppermute | solution.py:23
  60.0 48.7 %collective-permute-start.9 = (bf16[6,2,128,256]{3,2,1,0:T(8,128)(2,1)}, bf16[6,2,128,256]{3,2,1,0:T(8,128)(2,1)}, u32[]{:S(2)}, u32[]{:S(2)}) collective-permute-start(bf16[6,2,128,256]{3,2,1,0:T(8,128)(2,1)} %gate.12), channel_id=1, source_target_pairs={{0,4},{4,0},{8,12},{12,8},{1,5},{5,1},{9,13},{13,9},{2,6},{6,2},{1... | collective-permute-start | bytes 2359304 | tf_op jit(solution)/shard_map/ppermute | solution.py:23
  65.3 6.7 %collective-permute-start.1 = (bf16[2,128,256]{2,1,0:T(8,128)(2,1)}, bf16[2,128,256]{2,1,0:T(8,128)(2,1)S(1)}, u32[]{:S(2)}, u32[]{:S(2)}) collective-permute-start(bf16[2,128,256]{2,1,0:T(8,128)(2,1)} %get-tuple-element.55), channel_id=1, source_target_pairs={{0,16},{16,0},{1,17},{17,1},{2,18},{18,2},{3,19},{19,3},{4,20},{20... | collective-permute-start | bytes 393224 | tf_op jit(solution)/shard_map/cond/branch_1_fun/ppermute | solution.py:23
  66.6 4.1 %collective-permute-start = (f32[16,256]{1,0:T(8,128)}, f32[16,256]{1,0:T(8,128)S(1)}, u32[]{:S(2)}, u32[]{:S(2)}) collective-permute-start(f32[16,256]{1,0:T(8,128)} %get-tuple-element.54), channel_id=1, source_target_pairs={{0,16},{16,0},{1,17},{17,1},{2,18},{18,2},{3,19},{19,3},{4,20},{20... | collective-permute-start | bytes 49160 | tf_op jit(solution)/shard_map/cond/branch_1_fun/ppermute | solution.py:23
  72.0 0.6 copy-start.4
  72.7 26.1 %collective-permute-start.2 = (bf16[2,1024,256]{2,1,0:T(8,128)(2,1)}, bf16[2,1024,256]{2,1,0:T(8,128)(2,1)S(1)}, u32[]{:S(2)}, u32[]{:S(2)}) collective-permute-start(bf16[2,1024,256]{2,1,0:T(8,128)(2,1)} %gate.7), channel_id=1, source_target_pairs={{0,16},{16,0},{1,17},{17,1},{2,18},{18,2},{3,19},{19,3},{4,20},{20... | collective-permute-start | bytes 3145736 | tf_op jit(solution)/shard_map/cond/branch_1_fun/ppermute | solution.py:23
  74.0 1.4 %collective-permute-start.3 = (f32[16,256]{1,0:T(8,128)}, f32[16,256]{1,0:T(8,128)S(1)}, u32[]{:S(2)}, u32[]{:S(2)}) collective-permute-start(f32[16,256]{1,0:T(8,128)} %add.35.refs_1_), channel_id=1, source_target_pairs={{0,1},{1,0},{2,3},{3,2},{4,5},{5,4},{6,7},{7,6},{8,9},{9,8},{10,11... | collective-permute-start | bytes 49160 | tf_op jit(solution)/shard_map/cond/branch_1_fun/ppermute | solution.py:23
  76.1 3.7 %copy-start.8 = (f32[16,256]{1,0:T(8,128)}, f32[16,256]{1,0:T(8,128)S(1)}, u32[]{:S(2)}) copy-start(f32[16,256]{1,0:T(8,128)S(1)} %add.36.low_ref) | copy-start | bytes 49156 | tf_op jit(solution)/shard_map/cond
  76.1 3.7 %collective-permute-start.4 = (f32[16,256]{1,0:T(8,128)S(1)}, f32[16,256]{1,0:T(8,128)S(1)}, u32[]{:S(2)}, u32[]{:S(2)}) collective-permute-start(f32[16,256]{1,0:T(8,128)S(1)} %add.36.low_ref), channel_id=1, source_target_pairs={{0,2},{1,3},{2,0},{3,1},{4,6},{5,7},{6,4},{7,5},{8,10},{9,11},{10,... | collective-permute-start | bytes 49160 | tf_op jit(solution)/shard_map/cond/branch_1_fun/ppermute | solution.py:23
  79.8 0.6 copy-start.10
  89.3 19.4 %all-to-all-start = ((bf16[4,2,2,2560]{3,2,1,0:T(2,128)(2,1)}), bf16[4,2,2,2560]{3,2,1,0:T(2,128)(2,1)}, u32[]{:S(2)}, u32[]{:S(2)}) async-start(bf16[4,2,2,2560]{3,2,1,0:T(2,128)(2,1)} %bitcast.29), calls=%async_computation | async-start | bytes 163840 | tf_op jit(solution)/shard_map/cond/branch_1_fun/all_to_all | solution.py:597
  93.8 0.9 copy-start.1
  94.7 3.3 %copy-start.5 = (bf16[2,128,256]{2,1,0:T(8,128)(2,1)S(1)}, bf16[2,128,256]{2,1,0:T(8,128)(2,1)}, u32[]{:S(2)}) copy-start(bf16[2,128,256]{2,1,0:T(8,128)(2,1)} %copy-done.4) | copy-start | bytes 393220 | tf_op jit(solution)/shard_map/cond
  94.7 3.3 %copy-start.7 = (bf16[2,128,256]{2,1,0:T(8,128)(2,1)S(1)}, bf16[2,128,256]{2,1,0:T(8,128)(2,1)}, u32[]{:S(2)}) copy-start(bf16[2,128,256]{2,1,0:T(8,128)(2,1)} %get-tuple-element.63.ours_ref) | copy-start | bytes 393220 | tf_op jit(solution)/shard_map/cond
